TPU v7x, 32 devices: a whole 2x2x4 slice. The times are simulated.
32 devices in a mesh: cache: 8 (over z, y), cand: 4 (over x, core).
Axes of the slice: x: 2, y: 2, z: 4, core: 2. Of those that a mesh axis runs over, the one named last changes fastest.
Arguments:
- cand_states: bfloat16 [1024, 16, 1024], P('cand', 'cache'), may hold values from -6 to 6
- in_proj: bfloat16 [1024, 4, 1024], P(None, None, 'cand'), may hold values from -0.1875 to 0.1875
- out_proj: bfloat16 [1024, 1024], P('cand'), may hold values from -0.1875 to 0.1875
- history: bfloat16 [8, 16, 2, 512, 1024], P('cache', None, None, None, 'cand'), may hold values from -6 to 6
- lengths: int32 [16], replicated, may hold values from 2048 to 4096, as said below
- rank_users: int32 [16], replicated, may hold values from 0 to 15, each once
- recency_bias: float32 [8, 14], P('cand'), may hold values from -4 to 4
- score_weight: float32 [1024], replicated, may hold values from -0.1875 to 0.1875
Outputs:
- layer_out: bfloat16 [1024, 16, 1024], P('cand', 'cache')
- scores: float32 [1024, 16], P('cand', 'cache')
Inputs may be any that keep to these rules, and one draw needn't show every extreme that they name: `lengths`: every length is a multiple of 128; some user's length is exactly 4096. `rank_users`: each user is ranked in exactly one slot.
All inputs are finite; a program needn't handle non-finite values.
Results may differ from a plain program's by a relative error of at most 0.008.
Values may be sent and summed in bfloat16 or wider, within the bound.
No kernel may reach another device: no remote copies, remote signals or barrier semaphores. Data moves between devices by JAX's collectives and lax.ppermute only.
A program may use at most 128 MiB of HBM per device.

v0:
```python
import functools

import jax
import jax.numpy as jnp
from jax import lax
from jax.experimental import pallas as pl
from jax.experimental.pallas import tpu as pltpu
from jax.sharding import PartitionSpec as P

BLOCK = 128
EPSILON = 1e-06
MASKED = -1e30
MIB = 1024 * 1024
QUICK = pl.CostEstimate(flops=1, bytes_accessed=1, transcendentals=0)


def local_call(kernel, name, args, outs, scratch=(), places=(), held=True):
    places = dict(places)
    placed = [
        arg
        if places.get(i) == pltpu.SMEM
        else pltpu.with_memory_space_constraint(arg, places.get(i, pltpu.VMEM))
        for i, arg in enumerate(args)
    ]
    return pl.pallas_call(
        kernel,
        in_specs=[
            pl.BlockSpec(memory_space=places.get(i, pltpu.VMEM)) for i in range(len(args))
        ],
        out_specs=[pl.BlockSpec(memory_space=pltpu.VMEM)] * len(outs),
        out_shape=[
            pltpu.VMEM(shape, dtype) if held else jax.ShapeDtypeStruct(shape, dtype)
            for shape, dtype in outs
        ],
        scratch_shapes=list(scratch),
        compiler_params=pltpu.CompilerParams(vmem_limit_bytes=20 * MIB),
        cost_estimate=QUICK,
        name=name,
    )(*placed)


def tied(*arrays):
    return lax.optimization_barrier(arrays)


def bias_rows(recency_bias, most_blocks):
    bucket_count = recency_bias.shape[1]
    ends = jnp.arange(1, most_blocks + 1, dtype=jnp.int32)[:, None] * BLOCK
    distance = ends - jnp.arange(BLOCK, dtype=jnp.int32)[None, :]
    bucket = sum((distance >= 2**k).astype(jnp.int32) for k in range(bucket_count - 1))
    rows = sum(
        jnp.where(bucket[None] == b, recency_bias[:, b][:, None, None], 0.0)
        for b in range(bucket_count)
    )
    past = jnp.full((recency_bias.shape[0], 1, BLOCK), MASKED, jnp.float32)
    return jnp.concatenate([past, rows * 0.5], axis=1)


def attend_kernel(cache_count, step, member, halves, sends, picks, history, other, table, *refs):
    refs, (query, both, totals, sem, other_sem, next_sem) = refs[:-6], refs[-6:]
    queries, (out, *next_page) = (refs[:-2], refs[-2:]) if sends else (refs[:-1], refs[-1:])
    heads = table.shape[0]
    rows, width = out.shape
    size = width // heads
    blocks = both.shape[2] // BLOCK
    user, blocks_used, *shifts, which, next_user = (picks[6 * step + i] for i in range(6))
    fetch = pltpu.make_async_copy(history.at[0, user], both.at[0], sem)
    fetch.start()
    fetch_other = pltpu.make_async_copy(other.at[0], both.at[1], other_sem)
    fetch_other.start()
    if sends:
        next_fetch = pltpu.make_async_copy(history.at[0, next_user], next_page[0].at[0], next_sem)
        next_fetch.start()
    if len(queries) == halves:
        for i, ref in enumerate(queries):
            query[i * rows // halves : (i + 1) * rows // halves, :] = ref[...]
    else:
        for i, (first, second) in enumerate(zip(queries[:halves], queries[halves:])):
            query[i * rows // halves : (i + 1) * rows // halves, :] = jnp.where(
                which == 0, first[...], second[...]
            )

    chunk = min(2, blocks)
    needed = jnp.maximum(blocks_used - jnp.minimum(*shifts) + cache_count - 1, 0) // cache_count
    chunks = jnp.maximum((jnp.minimum(needed, blocks) + chunk - 1) // chunk, 1)

    def add_chunk(index, carry):
        page, first = 1 - index // chunks, index % chunks * chunk

        @pl.when(index == chunks)
        def _():
            fetch.wait()

        shift = jnp.where(page == 0, shifts[0], shifts[1])
        left = [
            jnp.maximum(blocks_used - ((first + i) * cache_count + shift), 0) for i in range(chunk)
        ]
        events = pl.ds(pl.multiple_of(first * BLOCK, BLOCK), chunk * BLOCK)
        for head in range(heads):
            columns = slice(head * size, (head + 1) * size)
            bias = jnp.concatenate([table[head, pl.ds(m, 1), :] for m in left], axis=1)
            half = bias + lax.dot_general(
                query[:, columns],
                both[page, 0, events, columns],
                (((1,), (1,)), ((), ())),
                preferred_element_type=jnp.float32,
            )
            weights = (half + half * jnp.tanh(half)).astype(jnp.bfloat16)
            totals[:, columns] += jnp.dot(
                weights, both[page, 1, events, columns], preferred_element_type=jnp.float32
            )
        return carry

    totals[...] = jnp.zeros_like(totals)
    fetch_other.wait()
    lax.fori_loop(0, 2 * chunks, add_chunk, 0)
    out[...] = totals[...].astype(jnp.bfloat16)

    if sends:
        next_fetch.wait()


def attend(cache_count, picks, step, queries, history, other, member, table, sends=False):
    halves = len(queries[0])
    queries = [piece for array in queries for piece in array]
    rows, width = halves * queries[0].shape[0], queries[0].shape[1]
    outs = [((rows, width), jnp.bfloat16), ((1,) + history.shape[2:], history.dtype)]
    return local_call(
        functools.partial(attend_kernel, cache_count, step, member, halves, sends),
        "attend",
        [picks, history, other, table, *queries],
        outs if sends else outs[:1],
        scratch=[
            pltpu.VMEM((rows, width), jnp.bfloat16),
            pltpu.VMEM((2,) + history.shape[2:], history.dtype),
            pltpu.VMEM((rows, width), jnp.float32),
            pltpu.SemaphoreType.DMA,
            pltpu.SemaphoreType.DMA,
            pltpu.SemaphoreType.DMA,
        ],
        places={0: pltpu.SMEM, 1: pltpu.HBM},
    )


def pages_kernel(users, history, *refs):
    outs, sem = refs[:-1], refs[-1]
    rows = min(2 * BLOCK, history.shape[3])
    copies = [
        pltpu.make_async_copy(
            history.at[0, users[i], kind, pl.ds(first, rows)],
            out.at[0, kind, pl.ds(first, rows)],
            sem.at[i, kind, first // rows],
        )
        for i, out in enumerate(outs)
        for kind in range(2)
        for first in range(0, history.shape[3], rows)
    ]
    for copy in copies:
        copy.start()
    for copy in copies:
        copy.wait()


def pages_of(users, count, history):
    return local_call(
        pages_kernel,
        "pages",
        [users, history],
        [((1,) + history.shape[2:], history.dtype)] * count,
        scratch=[pltpu.SemaphoreType.DMA((count, 2, max(1, history.shape[3] // (2 * BLOCK))))],
        places={0: pltpu.SMEM, 1: pltpu.HBM},
    )


def behind_kernel(scale, weight, ahead, *refs):
    *blocks, out = refs
    rows = ahead.shape[0]
    out[:rows, :] = ahead[...]
    project_kernel(
        [(2, scale)], 1, len(blocks), weight, *blocks, out.at[pl.ds(rows, rows)]
    )


def project_behind(ahead, scale, blocks, in_matrix):
    rows, width = ahead.shape
    (queries,) = local_call(
        functools.partial(behind_kernel, scale),
        "project",
        [in_matrix, ahead, *blocks],
        [((2 * rows, width), jnp.bfloat16)],
    )
    return queries


def project_kernel(kinds, groups, count, weight, *refs):
    blocks, outs = refs[:count], refs[count:]
    total, width = outs[0].shape
    first, group = 0, 0
    for block in blocks:
        rows = block.shape[0]
        state = block[...].astype(jnp.float32)
        half_norm = 0.5 * lax.rsqrt(jnp.mean(state * state, axis=-1, keepdims=True) + EPSILON)
        for (quarter, scale), out in zip(kinds, outs[group * len(kinds) :]):
            half = half_norm * jnp.dot(
                block[...],
                weight[:, quarter * width : (quarter + 1) * width],
                preferred_element_type=jnp.float32,
            )
            out[first : first + rows, :] = (
                (half + half * jnp.tanh(half)) * scale
            ).astype(jnp.bfloat16)
        first += rows
        if first == total:
            first, group = 0, group + 1


def project(kinds, blocks, in_matrix, groups=1):
    shape = (sum(block.shape[0] for block in blocks) // groups, in_matrix.shape[1] // 4)
    return local_call(
        functools.partial(project_kernel, kinds, groups, len(blocks)),
        "project",
        [in_matrix, *blocks],
        [(shape, jnp.bfloat16)] * (len(kinds) * groups),
    )


def finish_kernel(half, count, first_bias, *refs):
    parts, heads_refs, outs = refs[:count], refs[count:-2], refs[-2:]
    gates, values, keys, *queries = heads_refs
    heads = first_bias.shape[0]
    rows, width = outs[0].shape
    size = width // heads

    def load(ref, i, columns):
        first = i * rows
        if ref.shape[0] == 4 * rows:
            first = first + half * 2 * rows
        return ref[first : first + rows, columns].astype(jnp.float32)

    for i, out in enumerate(outs):
        for head in range(heads):
            columns = slice(head * size, (head + 1) * size)
            total = sum(load(part, i, columns) for part in parts)
            products = load(queries[0], i, columns) * load(keys, i, columns)
            score = jnp.sum(products, axis=-1, keepdims=True) + first_bias[head] * 0.5
            total = total + (score + score * jnp.tanh(score)) * load(values, i, columns)
            scale = lax.rsqrt(jnp.mean(total * total, axis=-1, keepdims=True) + EPSILON)
            out[:, columns] = (total * scale * load(gates, i, columns)).astype(jnp.bfloat16)


def finish(first_bias, half, parts, gates, values, keys, query):
    rows, width = gates.shape
    return local_call(
        functools.partial(finish_kernel, half, len(parts)),
        "finish",
        [first_bias, *parts, gates, values, keys, *query],
        [((rows // 4, width), jnp.bfloat16)] * 2,
        places={0: pltpu.SMEM},
    )


def combine_kernel(count, states, score_weight, *refs):
    gated, weights, rest = refs[:count], refs[count : 2 * count], refs[2 * count :]
    *before, layer, scores = rest
    total = states[...].astype(jnp.float32)
    for part, weight in zip(gated, weights):
        total = total + jnp.dot(part[...], weight[...], preferred_element_type=jnp.float32)
    column = jnp.sum(total * score_weight[...], axis=-1, keepdims=True)
    row = jnp.transpose(jnp.broadcast_to(column, (column.shape[0], 128)))[:1]
    if before:
        layer[:, 0, :] = before[0][...]
        layer[:, 1, :] = total.astype(jnp.bfloat16)
        scores[:1, :] = before[1][...]
        scores[1:, :] = row
    else:
        layer[...] = total.astype(jnp.bfloat16)
        scores[...] = row


def combine(states, score_weight, gated, weights, before=()):
    rows, width = states.shape
    layer = (rows, 2, width) if before else (rows, width)
    return local_call(
        functools.partial(combine_kernel, len(gated)),
        "combine",
        [states, score_weight[None], *gated, *weights, *before],
        [(layer, jnp.bfloat16), ((2 if before else 1, rows), jnp.float32)],
        held=False,
    )


def swap(axis, bit):
    return functools.partial(
        lax.ppermute, axis_name=axis, perm=[(i, i ^ bit) for i in range(lax.axis_size(axis))]
    )


def local(
    cand_states, in_proj, out_proj, history, lengths, rank_users, recency_bias, score_weight
):
    cache_count = lax.axis_size("cache")
    place = lax.axis_index("cache")
    cand_rows, users_here, width = cand_states.shape
    head_width = in_proj.shape[2]
    heads = recency_bias.shape[0]
    events = history.shape[3]
    half_scale = 0.5 * (head_width // heads) ** (-0.5)

    swap_core, swap_chip = swap("cand", 1), swap("cand", 2)
    swap_both = swap("cand", 3)
    swap_page = swap("cache", 1)

    states = jnp.moveaxis(cand_states, 1, 0)
    in_matrix = in_proj.reshape(width, 4 * head_width)
    table = bias_rows(recency_bias, cache_count * events // BLOCK)
    first_bias = recency_bias[:, 0]

    def lookup(values, places):
        index = jnp.arange(values.shape[0], dtype=jnp.int32)
        return jnp.sum(jnp.where(places[:, None] == index, values, 0), axis=1)

    def picks_of(users, first, second, which, others):
        used = lookup(lengths, users) // BLOCK
        columns = [
            users, used, jnp.remainder(first - users, cache_count),
            jnp.remainder(second - users, cache_count), jnp.broadcast_to(which, users.shape), others,
        ]
        return jnp.stack(columns, axis=1).reshape(-1).astype(jnp.int32)

    def spread(near, far):
        return [near[0], swap_core(near[1]), swap_chip(far[0]), swap_both(far[1])]

    if cache_count == 8 and users_here == 2:
        line = [
            [0, 1, 2, 3, 3, 2, 1, 0],
            [1, 2, 3, 0, 3, 2, 0, 1],
            [2, 1, 0, 3, 0, 1, 3, 2],
            [3, 2, 1, 0, 0, 1, 2, 3],
        ]
        slots = [
            [(line[p // 2][k] * 2 + q) * 2 + k // 4 for q in (1 - p % 2, p % 2) for k in range(8)]
            for p in range(8)
        ]
        slots = lax.dynamic_index_in_dim(jnp.array(slots, jnp.int32), place, 0, False)
        users = lookup(rank_users, slots)
        at_end = (place < 2) | (place >= 6)
        exchange_outer = swap("cache", 2)
        exchange_inner = functools.partial(
            lax.ppermute, axis_name="cache", perm=[(2, 4), (4, 2), (3, 5), (5, 3)]
        )
        picks = picks_of(
            users[8:], place, place ^ 1, jnp.where(at_end, 0, 1), jnp.roll(users[:8], -2)
        )
        query_only = ((2, half_scale),)
        all_others = ((0, 1.0), (1, 1.0), (3, 1.0))

        def either(first, second):
            return jnp.where(at_end, first, second)

        def heads_of(step, queries, pages, member=0, sends=False):
            return attend(
                cache_count, picks, step, queries, history, pages, member, table, sends
            )

        mine_a, mine_b = states[0], states[1]
        across_a, near_a, near_b = swap_chip(mine_a), swap_core(mine_a), swap_core(mine_b)
        mine_b, near_a = tied(mine_b, near_a)
        across_b = swap_chip(mine_b)
        waiting, sending = pages_of(users[:2], 2, history)
        page = swap_page(waiting)
        query_near_a, query_near_b = project(
            query_only, [mine_a, near_a, mine_b, near_b], in_matrix, groups=2
        )
        across_a, query_near_a = tied(across_a, query_near_a)
        rows_a = [mine_a, near_a, across_a, swap_core(across_a)]
        query_a = project_behind(query_near_a, half_scale, rows_a[2:], in_matrix)
        query_a, sending = tied(query_a, sending)

        outer, inner, totals = [], [], []
        for step in range(8):
            if step == 0:
                to_outer, to_inner, queries = query_a, query_a, [query_a]
            if step == 1:
                to_outer, to_inner = either(query_b, inner[0]), outer[0]
                queries = [outer[0], inner[0]]
            if step == 2:
                to_outer, to_inner = either(totals[1], inner[1]), outer[1]
                queries = [outer[1], inner[1]]
            if step == 3:
                to_outer, to_inner = either(totals[2], inner[2]), query_b
                queries = [outer[2], outer[0]]
                to_outer, out_mine = tied(to_outer, out_proj)
                out_across, out_near = swap_chip(out_mine), swap_core(out_mine)
            if step == 4:
                to_outer, to_inner = either(totals[3], inner[3]), outer[3] + totals[1]
                queries = [outer[3], inner[2]]
            if step == 5:
                to_outer, to_inner = either(totals[4], query_b), outer[4] + totals[2]
                queries = [outer[4], inner[3]]
            if step == 6:
                to_outer, to_inner = either(totals[5], inner[5] + totals[3]), outer[5] + totals[4]
                queries = [outer[5], outer[1]]
            if step == 7:
                to_outer, to_inner = either(totals[6], inner[6] + totals[6]), outer[6] + totals[5]
                queries = [query_b]
            held, page = page, swap_page(sending) if step < 7 else page
            outer.append(exchange_outer(to_outer))
            inner.append(exchange_inner(to_inner))
            total, *sending = heads_of(step, [[array] for array in queries], held, 0, step < 6)
            extra = []
            if step == 0:
                pieces = [swap_core(piece) for piece in jnp.split(across_b, 2)]
                rows_b = [mine_b, near_b, across_b, *pieces]
                extra = [project_behind(query_near_b, half_scale, rows_b[2:], in_matrix)]
            if step == 1:
                rows_a[0], total = tied(rows_a[0], total)
                extra = project(all_others, rows_a, in_matrix)
            if step == 2:
                rows_b[0], total = tied(rows_b[0], total)
                extra = project(all_others, rows_b, in_matrix)
            if step == 5:
                extra = [out_mine, out_near, out_across, swap_core(out_across)]
            if step == 7:
                parts_a = [totals[0], either(outer[6], outer[2]), inner[4]]
                far_a = finish(first_bias, 1, parts_a, *heads_a)
                near_a = finish(first_bias, 0, parts_a, *heads_a)
                extra = combine(states[0], score_weight, spread(near_a, far_a), out_rows)
            if step < 3:
                page, outer[step] = tied(page, outer[step])
            outer[step], inner[step], total, *rest = tied(
                outer[step], inner[step], total, *sending, *extra
            )
            totals.append(total)
            if sending:
                sending, *extra = rest
            else:
                extra = rest
            if step == 0:
                (query_b,) = extra
            if step == 0:
                (query_b,) = extra
            if step == 1:
                heads_a = (*extra, [query_a])
            if step == 2:
                heads_b = (*extra, [query_b])
            if step == 5:
                out_rows = extra
        parts_b = [totals[7], outer[7], inner[7]]
        far_b = finish(first_bias, 1, parts_b, *heads_b)
        near_b = finish(first_bias, 0, parts_b, *heads_b)
        layer, scores = combine(
            states[1], score_weight, spread(near_b, far_b), out_rows, extra
        )
        return layer, scores.T

    chosen = jnp.take(history[0], rank_users, axis=0).reshape(
        cache_count, users_here, 2, events, head_width
    )
    arrived = lax.all_to_all(chosen, "cache", split_axis=0, concat_axis=0, tiled=True)
    out_across = swap_chip(out_proj)
    weight_rows = [out_proj, swap_core(out_proj), out_across, swap_core(out_across)]
    my_users = lax.dynamic_slice_in_dim(rank_users, place * users_here, users_here)
    layers, scores = [], []
    for member in range(users_here):
        across = swap_chip(states[member])
        rows = [states[member], swap_core(states[member]), across, swap_core(across)]
        kinds = ((0, 1.0), (1, 1.0), (2, half_scale), (3, 1.0))
        gates, values, queries, keys = project(kinds, rows, in_matrix)

        def add_pair(step, total, member=member, queries=queries):
            pair = lax.dynamic_slice(
                arrived, (2 * step, member, 0, 0, 0), (2, 1, 2, events, head_width)
            )
            user = my_users[member][None]
            picks = picks_of(user, 2 * step, 2 * step + 1, 0, user).at[0].set(0)
            (part,) = attend(cache_count, picks, 0, [[queries]], pair[:1], pair[1:, 0], 0, table)
            return total + part.astype(jnp.float32)

        total = lax.fori_loop(
            0, cache_count // 2, add_pair, jnp.zeros(queries.shape, jnp.float32)
        )
        near, far = (
            finish(first_bias, half, [total], gates, values, keys, [queries]) for half in (0, 1)
        )
        layer, score = combine(states[member], score_weight, spread(near, far), weight_rows)
        layers.append(layer)
        scores.append(score)
    return jnp.stack(layers, axis=1), jnp.concatenate(scores, axis=0).T


def solution(mesh):
    in_specs = (
        P("cand", "cache", None),
        P(None, None, "cand"),
        P("cand", None),
        P("cache", None, None, None, "cand"),
        P(),
        P(),
        P("cand", None),
        P(),
    )
    out_specs = (P("cand", "cache", None), P("cand", "cache"))
    return jax.shard_map(local, mesh=mesh, in_specs=in_specs, out_specs=out_specs, check_vma=False)
```

profile of v0, /device:TPU:0, one launch (start us, length us, event | category | flops | bytes accessed | tf_op | source)
XLA Modules:
  0.0 150.6 jit_solution(4533551125530866320)
XLA Ops:
  0.6 1.5 copy.17
  2.8 2.6 %collective-permute-start = (bf16[256,1024]{1,0:T(8,128)(2,1)S(1)}, bf16[256,1024]{1,0:T(8,128)(2,1)}, u32[]{:S(2)}, u32[]{:S(2)}) collective-permute-start(bf16[256,1024]{1,0:T(8,128)(2,1)S(1)} %get-tuple-element.119.refs_0_.states), channel_id=1, source_target_pairs={{0,2},{1,3},{2,0},{3,1},{4,6},{5,7},{6,4},{7,5},{8,10},{9,11},{10,... | collective-permute-start | bytes 1572872 | tf_op jit(solution)/shard_map/ppermute | solution.py:366
  6.4 2.9 %pages.1 = (bf16[1,2,512,256]{3,2,1,0:T(8,128)(2,1)}, bf16[1,2,512,256]{3,2,1,0:T(8,128)(2,1)}) custom-call(s32[2]{0:T(128)S(1)} %bitcast.37, bf16[1,16,2,512,256]{4,3,2,1,0:T(8,128)(2,1)} %history.17), custom_call_target="tpu_custom_call" | custom-call | flops 1 | bytes 1 | tf_op jit(solution)/shard_map/pages/pallas_call | solution.py:25
  9.2 1.6 %collective-permute-start.7 = (bf16[1,2,512,256]{3,2,1,0:T(8,128)(2,1)}, bf16[1,2,512,256]{3,2,1,0:T(8,128)(2,1)}, u32[]{:S(2)}, u32[]{:S(2)}) collective-permute-start(bf16[1,2,512,256]{3,2,1,0:T(8,128)(2,1)} %get-tuple-element.106), channel_id=1, source_target_pairs={{0,4},{4,0},{8,12},{12,8},{16,20},{20,16},{24,28},{28,24},{1,5},{5... | collective-permute-start | bytes 1572872 | tf_op jit(solution)/shard_map/ppermute | solution.py:370
  10.8 2.1 %copy.15 = bf16[128,8,4,256]{3,1,2,0:T(8,128)(2,1)S(1)} copy(bf16[128,8,4,256]{3,2,1,0:T(4,128)(2,1)} %bitcast.40) | data formatting | bytes 4194304
  14.2 2.2 %project.5 = (bf16[512,256]{1,0:T(8,128)(2,1)S(1)}, bf16[512,256]{1,0:T(8,128)(2,1)S(1)}) custom-call(bf16[1024,1024]{1,0:T(8,128)(2,1)S(1)} %bitcast.30, bf16[256,1024]{1,0:T(8,128)(2,1)S(1)} %get-tuple-element.119.refs_0_.states, bf16[256,1024]{1,0:T(8,128)(2,1)} %collective-permute-done.1.refs_1_, ...), custom_call_target="tpu_custom_call" | custom-call | flops 1 | bytes 1 | tf_op jit(solution)/shard_map/project/pallas_call | solution.py:25
  16.4 1.8 %collective-permute-done.refs_0_.refs_2_ = bf16[256,1024]{1,0:T(8,128)(2,1)} collective-permute-done((bf16[256,1024]{1,0:T(8,128)(2,1)S(1)}, bf16[256,1024]{1,0:T(8,128)(2,1)}, u32[]{:S(2)}, u32[]{:S(2)}) %collective-permute-start) | collective-permute-done | bytes 524320 | tf_op jit(solution)/shard_map/ppermute | solution.py:366
  18.4 1.9 %collective-permute-done.3.refs_1_.refs_3_ = bf16[256,1024]{1,0:T(8,128)(2,1)S(1)} collective-permute-done((bf16[256,1024]{1,0:T(8,128)(2,1)}, bf16[256,1024]{1,0:T(8,128)(2,1)S(1)}, u32[]{:S(2)}, u32[]{:S(2)}) %collective-permute-start.3) | collective-permute-done | bytes 524320 | tf_op jit(solution)/shard_map/ppermute | solution.py:375
  20.3 1.8 %project.6.refs_0_.refs_6_ = bf16[1024,256]{1,0:T(8,128)(2,1)S(1)} custom-call(bf16[1024,1024]{1,0:T(8,128)(2,1)S(1)} %bitcast.31, bf16[512,256]{1,0:T(8,128)(2,1)S(1)} %get-tuple-element.100.ahead, bf16[256,1024]{1,0:T(8,128)(2,1)} %collective-permute-done.refs_0_.refs_2_, bf16[256,1024]{1,0:T(8,128)(2,1)S(1)} %collective-permute-done.3.refs_1_.refs_3_), custom_call_target="tpu_custom_call" | custom-call | flops 1 | bytes 1 | tf_op jit(solution)/shard_map/project/pallas_call | solution.py:25
  22.1 2.1 %collective-permute-start.5 = (bf16[1024,256]{1,0:T(8,128)(2,1)S(1)}, bf16[1024,256]{1,0:T(8,128)(2,1)}, u32[]{:S(2)}, u32[]{:S(2)}) collective-permute-start(bf16[1024,256]{1,0:T(8,128)(2,1)S(1)} %project.6.refs_0_.refs_6_), channel_id=1, source_target_pairs={{0,8},{4,12},{8,0},{12,4},{16,24},{20,28},{24,16},{28,20},{1,9},{5... | collective-permute-start | bytes 1572872 | tf_op jit(solution)/shard_map/ppermute | solution.py:407
  25.7 1.5 %collective-permute-start.4 = (bf16[1,2,512,256]{3,2,1,0:T(8,128)(2,1)}, bf16[1,2,512,256]{3,2,1,0:T(8,128)(2,1)}, u32[]{:S(2)}, u32[]{:S(2)}) collective-permute-start(bf16[1,2,512,256]{3,2,1,0:T(8,128)(2,1)} %get-tuple-element.103), channel_id=1, source_target_pairs={{0,4},{4,0},{8,12},{12,8},{16,20},{20,16},{24,28},{28,24},{1,5},{5... | collective-permute-start | bytes 1572872 | tf_op jit(solution)/shard_map/ppermute | solution.py:406
  27.2 1.9 %collective-permute-done.8.refs_0_.refs_2_ = bf16[256,1024]{1,0:T(8,128)(2,1)S(1)} collective-permute-done((bf16[256,1024]{1,0:T(8,128)(2,1)S(1)}, bf16[256,1024]{1,0:T(8,128)(2,1)S(1)}, u32[]{:S(2)}, u32[]{:S(2)}) %collective-permute-start.8) | collective-permute-done | bytes 524320 | tf_op jit(solution)/shard_map/ppermute | solution.py:368
  31.7 4.7 %attend.8 = (bf16[1024,256]{1,0:T(8,128)(2,1)S(1)}, bf16[1,2,512,256]{3,2,1,0:T(8,128)(2,1)S(1)}) custom-call(s32[48]{0:T(128)S(1)} %reshape.389.picks, bf16[1,16,2,512,256]{4,3,2,1,0:T(8,128)(2,1)} %history.17, bf16[1,2,512,256]{3,2,1,0:T(8,128)(2,1)} %collective-permute-done.7.other, f32[2,33,128]{2,1,0:T(8,128)S(1)} %concatenate.8.table, ...), custom_call_target="tpu_custom_call" | custom-call | flops 1 | bytes 1 | tf_op jit(solution)/shard_map/attend/pallas_call | solution.py:25
  36.4 1.5 %project.7.refs_0_.refs_6_ = bf16[1024,256]{1,0:T(8,128)(2,1)S(1)} custom-call(bf16[1024,1024]{1,0:T(8,128)(2,1)S(1)} %bitcast.32, bf16[512,256]{1,0:T(8,128)(2,1)S(1)} %copy-done.8, bf16[256,1024]{1,0:T(8,128)(2,1)S(1)} %copy-done.3, bf16[128,1024]{1,0:T(8,128)(2,1)} %collective-permute-done.9.refs_1_.refs_3_, ...), custom_call_target="tpu_custom_call" | custom-call | flops 1 | bytes 1 | tf_op jit(solution)/shard_map/project/pallas_call | solution.py:25
  37.9 1.8 %collective-permute-done.4.other = bf16[1,2,512,256]{3,2,1,0:T(8,128)(2,1)} collective-permute-done((bf16[1,2,512,256]{3,2,1,0:T(8,128)(2,1)}, bf16[1,2,512,256]{3,2,1,0:T(8,128)(2,1)}, u32[]{:S(2)}, u32[]{:S(2)}) %collective-permute-start.4) | collective-permute-done | bytes 524320 | tf_op jit(solution)/shard_map/ppermute | solution.py:406
  39.8 4.5 %collective-permute-start.12 = (bf16[1024,256]{1,0:T(8,128)(2,1)S(1)}, bf16[1024,256]{1,0:T(8,128)(2,1)S(1)}, u32[]{:S(2)}, u32[]{:S(2)}) collective-permute-start(bf16[1024,256]{1,0:T(8,128)(2,1)S(1)} %broadcast_select_fusion.5), channel_id=1, source_target_pairs={{0,8},{4,12},{8,0},{12,4},{16,24},{20,28},{24,16},{28,20},{1,9},{5... | collective-permute-start | bytes 1572872 | tf_op jit(solution)/shard_map/ppermute | solution.py:407
  44.3 1.5 %collective-permute-start.11 = (bf16[1,2,512,256]{3,2,1,0:T(8,128)(2,1)S(1)}, bf16[1,2,512,256]{3,2,1,0:T(8,128)(2,1)S(1)}, u32[]{:S(2)}, u32[]{:S(2)}) collective-permute-start(bf16[1,2,512,256]{3,2,1,0:T(8,128)(2,1)S(1)} %get-tuple-element.110), channel_id=1, source_target_pairs={{0,4},{4,0},{8,12},{12,8},{16,20},{20,16},{24,28},{28,24},{1,5},{5... | collective-permute-start | bytes 1572872 | tf_op jit(solution)/shard_map/ppermute | solution.py:406
  46.5 3.3 %attend.9 = (bf16[1024,256]{1,0:T(8,128)(2,1)S(1)}, bf16[1,2,512,256]{3,2,1,0:T(8,128)(2,1)S(1)}) custom-call(s32[48]{0:T(128)S(1)} %reshape.389.picks, bf16[1,16,2,512,256]{4,3,2,1,0:T(8,128)(2,1)} %history.17, bf16[1,2,512,256]{3,2,1,0:T(8,128)(2,1)} %collective-permute-done.4.other, f32[2,33,128]{2,1,0:T(8,128)S(1)} %concatenate.8.table, ...), custom_call_target="tpu_custom_call" | custom-call | flops 1 | bytes 1 | tf_op jit(solution)/shard_map/attend/pallas_call | solution.py:25
  49.8 3.4 %project.8 = (bf16[1024,256]{1,0:T(8,128)(2,1)S(1)}, bf16[1024,256]{1,0:T(8,128)(2,1)S(1)}, bf16[1024,256]{1,0:T(8,128)(2,1)S(1)}) custom-call(bf16[1024,1024]{1,0:T(8,128)(2,1)S(1)} %bitcast.33, bf16[256,1024]{1,0:T(8,128)(2,1)S(1)} %copy-done.1, bf16[256,1024]{1,0:T(8,128)(2,1)} %collective-permute-done.1.refs_1_, ...), custom_call_target="tpu_custom_call" | custom-call | flops 1 | bytes 1 | tf_op jit(solution)/shard_map/project/pallas_call | solution.py:25
  53.3 1.8 %collective-permute-done.12.refs_0_.refs_1_ = bf16[1024,256]{1,0:T(8,128)(2,1)S(1)} collective-permute-done((bf16[1024,256]{1,0:T(8,128)(2,1)S(1)}, bf16[1024,256]{1,0:T(8,128)(2,1)S(1)}, u32[]{:S(2)}, u32[]{:S(2)}) %collective-permute-start.12) | collective-permute-done | bytes 524320 | tf_op jit(solution)/shard_map/ppermute | solution.py:407
  55.0 1.5 collective-permute-done.11.other
  56.5 3.8 %collective-permute-start.15 = (bf16[1024,256]{1,0:T(8,128)(2,1)S(1)}, bf16[1024,256]{1,0:T(8,128)(2,1)S(1)}, u32[]{:S(2)}, u32[]{:S(2)}) collective-permute-start(bf16[1024,256]{1,0:T(8,128)(2,1)S(1)} %broadcast_select_fusion.4), channel_id=1, source_target_pairs={{0,8},{4,12},{8,0},{12,4},{16,24},{20,28},{24,16},{28,20},{1,9},{5... | collective-permute-start | bytes 1572872 | tf_op jit(solution)/shard_map/ppermute | solution.py:407
  62.2 2.7 %attend.10 = (bf16[1024,256]{1,0:T(8,128)(2,1)S(1)}, bf16[1,2,512,256]{3,2,1,0:T(8,128)(2,1)S(1)}) custom-call(s32[48]{0:T(128)S(1)} %reshape.389.picks, bf16[1,16,2,512,256]{4,3,2,1,0:T(8,128)(2,1)} %history.17, bf16[1,2,512,256]{3,2,1,0:T(8,128)(2,1)S(1)} %collective-permute-done.11.other, f32[2,33,128]{2,1,0:T(8,128)S(1)} %concatenate.8.table, ...), custom_call_target="tpu_custom_call" | custom-call | flops 1 | bytes 1 | tf_op jit(solution)/shard_map/attend/pallas_call | solution.py:25
  64.9 3.5 %project.9 = (bf16[1024,256]{1,0:T(8,128)(2,1)S(1)}, bf16[1024,256]{1,0:T(8,128)(2,1)S(1)}, bf16[1024,256]{1,0:T(8,128)(2,1)S(1)}) custom-call(bf16[1024,1024]{1,0:T(8,128)(2,1)S(1)} %bitcast.34, bf16[256,1024]{1,0:T(8,128)(2,1)S(1)} %get-tuple-element.132.refs_2_.refs_0_.states, bf16[256,1024]{1,0:T(8,128)(2,1)} %collective-permute-done.2.refs_3_.refs_1_, ...), custom_call_target="tpu_custom_call" | custom-call | flops 1 | bytes 1 | tf_op jit(solution)/shard_map/project/pallas_call | solution.py:25
  68.3 1.5 collective-permute-done.15.refs_0_
  69.8 1.5 collective-permute-done.14.other
  71.4 6.4 %collective-permute-start.17 = (bf16[1024,256]{1,0:T(8,128)(2,1)S(1)}, bf16[1024,256]{1,0:T(8,128)(2,1)S(1)}, u32[]{:S(2)}, u32[]{:S(2)}) collective-permute-start(bf16[1024,256]{1,0:T(8,128)(2,1)S(1)} %broadcast_select_fusion.3), channel_id=1, source_target_pairs={{0,8},{4,12},{8,0},{12,4},{16,24},{20,28},{24,16},{28,20},{1,9},{5... | collective-permute-start | bytes 1572872 | tf_op jit(solution)/shard_map/ppermute | solution.py:407
  77.8 1.5 %collective-permute-start.21 = (bf16[1,2,512,256]{3,2,1,0:T(8,128)(2,1)S(1)}, bf16[1,2,512,256]{3,2,1,0:T(8,128)(2,1)S(1)}, u32[]{:S(2)}, u32[]{:S(2)}) collective-permute-start(bf16[1,2,512,256]{3,2,1,0:T(8,128)(2,1)S(1)} %get-tuple-element.146), channel_id=1, source_target_pairs={{0,4},{4,0},{8,12},{12,8},{16,20},{20,16},{24,28},{28,24},{1,5},{5... | collective-permute-start | bytes 1572872 | tf_op jit(solution)/shard_map/ppermute | solution.py:406
  79.3 1.5 collective-permute-start.26
  80.8 4.6 %attend.11 = (bf16[1024,256]{1,0:T(8,128)(2,1)S(1)}, bf16[1,2,512,256]{3,2,1,0:T(8,128)(2,1)S(1)}) custom-call(s32[48]{0:T(128)S(1)} %reshape.389.picks, bf16[1,16,2,512,256]{4,3,2,1,0:T(8,128)(2,1)} %history.17, bf16[1,2,512,256]{3,2,1,0:T(8,128)(2,1)S(1)} %collective-permute-done.14.other, f32[2,33,128]{2,1,0:T(8,128)S(1)} %concatenate.8.table, ...), custom_call_target="tpu_custom_call" | custom-call | flops 1 | bytes 1 | tf_op jit(solution)/shard_map/attend/pallas_call | solution.py:25
  86.3 3.4 %collective-permute-start.19 = (bf16[1024,256]{1,0:T(8,128)(2,1)S(1)}, bf16[1024,256]{1,0:T(8,128)(2,1)S(1)}, u32[]{:S(2)}, u32[]{:S(2)}) collective-permute-start(bf16[1024,256]{1,0:T(8,128)(2,1)S(1)} %broadcast_select_fusion.2), channel_id=1, source_target_pairs={{0,8},{4,12},{8,0},{12,4},{16,24},{20,28},{24,16},{28,20},{1,9},{5... | collective-permute-start | bytes 1572872 | tf_op jit(solution)/shard_map/ppermute | solution.py:407
  89.7 1.5 %collective-permute-start.24 = (bf16[1,2,512,256]{3,2,1,0:T(8,128)(2,1)S(1)}, bf16[1,2,512,256]{3,2,1,0:T(8,128)(2,1)S(1)}, u32[]{:S(2)}, u32[]{:S(2)}) collective-permute-start(bf16[1,2,512,256]{3,2,1,0:T(8,128)(2,1)S(1)} %get-tuple-element.151), channel_id=1, source_target_pairs={{0,4},{4,0},{8,12},{12,8},{16,20},{20,16},{24,28},{28,24},{1,5},{5... | collective-permute-start | bytes 1572872 | tf_op jit(solution)/shard_map/ppermute | solution.py:406
  91.3 4.1 %attend.12 = (bf16[1024,256]{1,0:T(8,128)(2,1)S(1)}, bf16[1,2,512,256]{3,2,1,0:T(8,128)(2,1)S(1)}) custom-call(s32[48]{0:T(128)S(1)} %reshape.389.picks, bf16[1,16,2,512,256]{4,3,2,1,0:T(8,128)(2,1)} %history.17, bf16[1,2,512,256]{3,2,1,0:T(8,128)(2,1)S(1)} %collective-permute-done.21.other, f32[2,33,128]{2,1,0:T(8,128)S(1)} %concatenate.8.table, ...), custom_call_target="tpu_custom_call" | custom-call | flops 1 | bytes 1 | tf_op jit(solution)/shard_map/attend/pallas_call | solution.py:25
  97.8 4.7 %collective-permute-start.22 = (bf16[1024,256]{1,0:T(8,128)(2,1)S(1)}, bf16[1024,256]{1,0:T(8,128)(2,1)S(1)}, u32[]{:S(2)}, u32[]{:S(2)}) collective-permute-start(bf16[1024,256]{1,0:T(8,128)(2,1)S(1)} %broadcast_select_fusion.1), channel_id=1, source_target_pairs={{0,8},{4,12},{8,0},{12,4},{16,24},{20,28},{24,16},{28,20},{1,9},{5... | collective-permute-start | bytes 1572872 | tf_op jit(solution)/shard_map/ppermute | solution.py:407
  102.5 1.6 %collective-permute-done.24.other = bf16[1,2,512,256]{3,2,1,0:T(8,128)(2,1)S(1)} collective-permute-done((bf16[1,2,512,256]{3,2,1,0:T(8,128)(2,1)S(1)}, bf16[1,2,512,256]{3,2,1,0:T(8,128)(2,1)S(1)}, u32[]{:S(2)}, u32[]{:S(2)}) %collective-permute-start.24) | collective-permute-done | bytes 524320 | tf_op jit(solution)/shard_map/ppermute | solution.py:406
  104.1 1.5 %collective-permute-start.30 = (bf16[1,2,512,256]{3,2,1,0:T(8,128)(2,1)S(1)}, bf16[1,2,512,256]{3,2,1,0:T(8,128)(2,1)S(1)}, u32[]{:S(2)}, u32[]{:S(2)}) collective-permute-start(bf16[1,2,512,256]{3,2,1,0:T(8,128)(2,1)S(1)} %get-tuple-element.158), channel_id=1, source_target_pairs={{0,4},{4,0},{8,12},{12,8},{16,20},{20,16},{24,28},{28,24},{1,5},{5... | collective-permute-start | bytes 1572872 | tf_op jit(solution)/shard_map/ppermute | solution.py:406
  105.6 4.1 %attend.13 = (bf16[1024,256]{1,0:T(8,128)(2,1)S(1)}, bf16[1,2,512,256]{3,2,1,0:T(8,128)(2,1)S(1)}) custom-call(s32[48]{0:T(128)S(1)} %reshape.389.picks, bf16[1,16,2,512,256]{4,3,2,1,0:T(8,128)(2,1)} %history.17, bf16[1,2,512,256]{3,2,1,0:T(8,128)(2,1)S(1)} %collective-permute-done.24.other, f32[2,33,128]{2,1,0:T(8,128)S(1)} %concatenate.8.table, ...), custom_call_target="tpu_custom_call" | custom-call | flops 1 | bytes 1 | tf_op jit(solution)/shard_map/attend/pallas_call | solution.py:25
  109.7 1.8 %collective-permute-done.22.refs_0_ = bf16[1024,256]{1,0:T(8,128)(2,1)S(1)} collective-permute-done((bf16[1024,256]{1,0:T(8,128)(2,1)S(1)}, bf16[1024,256]{1,0:T(8,128)(2,1)S(1)}, u32[]{:S(2)}, u32[]{:S(2)}) %collective-permute-start.22) | collective-permute-done | bytes 524320 | tf_op jit(solution)/shard_map/ppermute | solution.py:407
  112.4 3.6 %collective-permute-start.28 = (bf16[1024,256]{1,0:T(8,128)(2,1)S(1)}, bf16[1024,256]{1,0:T(8,128)(2,1)S(1)}, u32[]{:S(2)}, u32[]{:S(2)}) collective-permute-start(bf16[1024,256]{1,0:T(8,128)(2,1)S(1)} %add_select_fusion.1), channel_id=1, source_target_pairs={{0,8},{4,12},{8,0},{12,4},{16,24},{20,28},{24,16},{28,20},{1,9},{5... | collective-permute-start | bytes 1572872 | tf_op jit(solution)/shard_map/ppermute | solution.py:407
  116.6 2.3 %collective-permute-done.30.other = bf16[1,2,512,256]{3,2,1,0:T(8,128)(2,1)S(1)} collective-permute-done((bf16[1,2,512,256]{3,2,1,0:T(8,128)(2,1)S(1)}, bf16[1,2,512,256]{3,2,1,0:T(8,128)(2,1)S(1)}, u32[]{:S(2)}, u32[]{:S(2)}) %collective-permute-start.30) | collective-permute-done | bytes 524320 | tf_op jit(solution)/shard_map/ppermute | solution.py:406
  118.9 4.1 %attend.14 = bf16[1024,256]{1,0:T(8,128)(2,1)S(1)} custom-call(s32[48]{0:T(128)S(1)} %reshape.389.picks, bf16[1,16,2,512,256]{4,3,2,1,0:T(8,128)(2,1)} %history.17, bf16[1,2,512,256]{3,2,1,0:T(8,128)(2,1)S(1)} %collective-permute-done.30.other, f32[2,33,128]{2,1,0:T(8,128)S(1)} %concatenate.8.table, bf16[1024,256]{1,0:T(8,128)(2,1)S(1)} %collective-permute-done.22.refs_0_, ...), custom_call_target="tpu_custom_call" | custom-call | flops 1 | bytes 1 | tf_op jit(solution)/shard_map/attend/pallas_call | solution.py:25
  123.0 1.6 %collective-permute-done.28 = bf16[1024,256]{1,0:T(8,128)(2,1)S(1)} collective-permute-done((bf16[1024,256]{1,0:T(8,128)(2,1)S(1)}, bf16[1024,256]{1,0:T(8,128)(2,1)S(1)}, u32[]{:S(2)}, u32[]{:S(2)}) %collective-permute-start.28) | collective-permute-done | bytes 524320 | tf_op jit(solution)/shard_map/ppermute | solution.py:407
  125.5 3.7 %collective-permute-start.31 = (bf16[1024,256]{1,0:T(8,128)(2,1)S(1)}, bf16[1024,256]{1,0:T(8,128)(2,1)S(1)}, u32[]{:S(2)}, u32[]{:S(2)}) collective-permute-start(bf16[1024,256]{1,0:T(8,128)(2,1)S(1)} %add_select_fusion), channel_id=1, source_target_pairs={{0,8},{4,12},{8,0},{12,4},{16,24},{20,28},{24,16},{28,20},{1,9},{5... | collective-permute-start | bytes 1572872 | tf_op jit(solution)/shard_map/ppermute | solution.py:407
  131.3 1.6 %collective-permute-start.35 = (bf16[256,256]{1,0:T(8,128)(2,1)S(1)}, bf16[256,256]{1,0:T(8,128)(2,1)S(1)}, u32[]{:S(2)}, u32[]{:S(2)}) collective-permute-start(bf16[256,256]{1,0:T(8,128)(2,1)S(1)} %get-tuple-element.170), channel_id=1, source_target_pairs={{0,2},{1,3},{2,0},{3,1},{4,6},{5,7},{6,4},{7,5},{8,10},{9,11},{10,... | collective-permute-start | bytes 393224 | tf_op jit(solution)/shard_map/ppermute | solution.py:331
  133.5 4.3 %attend.15.refs_0_ = bf16[1024,256]{1,0:T(8,128)(2,1)S(1)} custom-call(s32[48]{0:T(128)S(1)} %reshape.389.picks, bf16[1,16,2,512,256]{4,3,2,1,0:T(8,128)(2,1)} %history.17, bf16[1,2,512,256]{3,2,1,0:T(8,128)(2,1)S(1)} %collective-permute-done.33.other, f32[2,33,128]{2,1,0:T(8,128)S(1)} %concatenate.8.table, bf16[1024,256]{1,0:T(8,128)(2,1)S(1)} %project.7.refs_0_.refs_6_), custom_call_target="tpu_custom_call" | custom-call | flops 1 | bytes 1 | tf_op jit(solution)/shard_map/attend/pallas_call | solution.py:25
  143.9 3.0 %collective-permute-done.38.refs_2_ = bf16[256,256]{1,0:T(8,128)(2,1)S(1)} collective-permute-done((bf16[256,256]{1,0:T(8,128)(2,1)S(1)}, bf16[256,256]{1,0:T(8,128)(2,1)S(1)}, u32[]{:S(2)}, u32[]{:S(2)}) %collective-permute-start.38) | collective-permute-done | bytes 131104 | tf_op jit(solution)/shard_map/ppermute | solution.py:331
  147.0 1.6 %collective-permute-done.39.refs_3_ = bf16[256,256]{1,0:T(8,128)(2,1)S(1)} collective-permute-done((bf16[256,256]{1,0:T(8,128)(2,1)S(1)}, bf16[256,256]{1,0:T(8,128)(2,1)S(1)}, u32[]{:S(2)}, u32[]{:S(2)}) %collective-permute-start.39) | collective-permute-done | bytes 131104 | tf_op jit(solution)/shard_map/ppermute | solution.py:331
  148.6 2.0 %combine.3 = (bf16[256,2,1024]{2,1,0:T(2,128)(2,1)}, f32[2,256]{1,0:T(2,128)}) custom-call(bf16[256,1024]{1,0:T(8,128)(2,1)S(1)} %get-tuple-element.132.refs_2_.refs_0_.states, f32[1,1024]{1,0:T(1,128)S(1)} %bitcast.36, bf16[256,256]{1,0:T(8,128)(2,1)S(1)} %get-tuple-element.184.refs_0_, bf16[256,256]{1,0:T(8,128)(2,1)S(1)} %collective-permute-done.37.refs_1_, ...), custom_call_target="tpu_custom_call" | custom-call | flops 1 | bytes 1 | tf_op jit(solution)/shard_map/combine/pallas_call | solution.py:25
  (109 shorter events, 24.4 us)
Async XLA Ops:
  0.6 5.5 %copy-start.11 = (s32[16]{0:T(128)S(1)}, s32[16]{0:T(128)}, u32[]{:S(2)}) copy-start(s32[16]{0:T(128)} %param.14) | copy-start | bytes 196
  2.2 12.0 %copy-start = (bf16[256,1024]{1,0:T(8,128)(2,1)}, bf16[256,1024]{1,0:T(8,128)(2,1)S(1)}, u32[]{:S(2)}) copy-start(bf16[256,1024]{1,0:T(8,128)(2,1)S(1)} %get-tuple-element.119.refs_0_.states) | copy-start | bytes 1572868
  2.2 11.4 %collective-permute-start.1 = (bf16[256,1024]{1,0:T(8,128)(2,1)S(1)}, bf16[256,1024]{1,0:T(8,128)(2,1)}, u32[]{:S(2)}, u32[]{:S(2)}) collective-permute-start(bf16[256,1024]{1,0:T(8,128)(2,1)S(1)} %get-tuple-element.119.refs_0_.states), channel_id=1, source_target_pairs={{0,1},{1,0},{2,3},{3,2},{4,5},{5,4},{6,7},{7,6},{8,9},{9,8},{10,11... | collective-permute-start | bytes 1572872 | tf_op jit(solution)/shard_map/ppermute | solution.py:366
  2.8 15.4 %collective-permute-start = (bf16[256,1024]{1,0:T(8,128)(2,1)S(1)}, bf16[256,1024]{1,0:T(8,128)(2,1)}, u32[]{:S(2)}, u32[]{:S(2)}) collective-permute-start(bf16[256,1024]{1,0:T(8,128)(2,1)S(1)} %get-tuple-element.119.refs_0_.states), channel_id=1, source_target_pairs={{0,2},{1,3},{2,0},{3,1},{4,6},{5,7},{6,4},{7,5},{8,10},{9,11},{10,... | collective-permute-start | bytes 1572872 | tf_op jit(solution)/shard_map/ppermute | solution.py:366
  5.3 8.9 %collective-permute-start.2 = (bf16[256,1024]{1,0:T(8,128)(2,1)S(1)}, bf16[256,1024]{1,0:T(8,128)(2,1)}, u32[]{:S(2)}, u32[]{:S(2)}) collective-permute-start(bf16[256,1024]{1,0:T(8,128)(2,1)S(1)} %get-tuple-element.132.refs_2_.refs_0_.states), channel_id=1, source_target_pairs={{0,1},{1,0},{2,3},{3,2},{4,5},{5,4},{6,7},{7,6},{8,9},{9,8},{10,11... | collective-permute-start | bytes 1572872 | tf_op jit(solution)/shard_map/ppermute | solution.py:366
  9.2 21.5 %collective-permute-start.7 = (bf16[1,2,512,256]{3,2,1,0:T(8,128)(2,1)}, bf16[1,2,512,256]{3,2,1,0:T(8,128)(2,1)}, u32[]{:S(2)}, u32[]{:S(2)}) collective-permute-start(bf16[1,2,512,256]{3,2,1,0:T(8,128)(2,1)} %get-tuple-element.106), channel_id=1, source_target_pairs={{0,4},{4,0},{8,12},{12,8},{16,20},{20,16},{24,28},{28,24},{1,5},{5... | collective-permute-start | bytes 1572872 | tf_op jit(solution)/shard_map/ppermute | solution.py:370
  13.6 15.5 %collective-permute-start.8 = (bf16[256,1024]{1,0:T(8,128)(2,1)S(1)}, bf16[256,1024]{1,0:T(8,128)(2,1)S(1)}, u32[]{:S(2)}, u32[]{:S(2)}) collective-permute-start(bf16[256,1024]{1,0:T(8,128)(2,1)S(1)} %get-tuple-element.132.refs_2_.refs_0_.states), channel_id=1, source_target_pairs={{0,2},{1,3},{2,0},{3,1},{4,6},{5,7},{6,4},{7,5},{8,10},{9,11},{10,... | collective-permute-start | bytes 1572872 | tf_op jit(solution)/shard_map/ppermute | solution.py:368
  16.4 13.5 %copy-start.7 = (bf16[512,256]{1,0:T(8,128)(2,1)}, bf16[512,256]{1,0:T(8,128)(2,1)S(1)}, u32[]{:S(2)}) copy-start(bf16[512,256]{1,0:T(8,128)(2,1)S(1)} %get-tuple-element.109.ahead) | copy-start | bytes 786436
  18.2 2.1 %collective-permute-start.3 = (bf16[256,1024]{1,0:T(8,128)(2,1)}, bf16[256,1024]{1,0:T(8,128)(2,1)S(1)}, u32[]{:S(2)}, u32[]{:S(2)}) collective-permute-start(bf16[256,1024]{1,0:T(8,128)(2,1)} %collective-permute-done.refs_0_.refs_2_), channel_id=1, source_target_pairs={{0,1},{1,0},{2,3},{3,2},{4,5},{5,4},{6,7},{7,6},{8,9},{9,8},{10,11... | collective-permute-start | bytes 1572872 | tf_op jit(solution)/shard_map/ppermute | solution.py:375
  20.3 9.6 %copy-start.5 = (bf16[256,1024]{1,0:T(8,128)(2,1)}, bf16[256,1024]{1,0:T(8,128)(2,1)S(1)}, u32[]{:S(2)}) copy-start(bf16[256,1024]{1,0:T(8,128)(2,1)S(1)} %collective-permute-done.3.refs_1_.refs_3_) | copy-start | bytes 1572868
  22.1 15.8 %collective-permute-start.5 = (bf16[1024,256]{1,0:T(8,128)(2,1)S(1)}, bf16[1024,256]{1,0:T(8,128)(2,1)}, u32[]{:S(2)}, u32[]{:S(2)}) collective-permute-start(bf16[1024,256]{1,0:T(8,128)(2,1)S(1)} %project.6.refs_0_.refs_6_), channel_id=1, source_target_pairs={{0,8},{4,12},{8,0},{12,4},{16,24},{20,28},{24,16},{28,20},{1,9},{5... | collective-permute-start | bytes 1572872 | tf_op jit(solution)/shard_map/ppermute | solution.py:407
  24.2 15.5 %collective-permute-start.6 = (bf16[1024,256]{1,0:T(8,128)(2,1)S(1)}, bf16[1024,256]{1,0:T(8,128)(2,1)}, u32[]{:S(2)}, u32[]{:S(2)}) collective-permute-start(bf16[1024,256]{1,0:T(8,128)(2,1)S(1)} %project.6.refs_0_.refs_6_), channel_id=1, source_target_pairs={{8,16},{16,8},{12,20},{20,12},{9,17},{17,9},{13,21},{21,13},{10,18... | collective-permute-start | bytes 1572872 | tf_op jit(solution)/shard_map/ppermute | solution.py:408
  25.7 14.0 %collective-permute-start.4 = (bf16[1,2,512,256]{3,2,1,0:T(8,128)(2,1)}, bf16[1,2,512,256]{3,2,1,0:T(8,128)(2,1)}, u32[]{:S(2)}, u32[]{:S(2)}) collective-permute-start(bf16[1,2,512,256]{3,2,1,0:T(8,128)(2,1)} %get-tuple-element.103), channel_id=1, source_target_pairs={{0,4},{4,0},{8,12},{12,8},{16,20},{20,16},{24,28},{28,24},{1,5},{5... | collective-permute-start | bytes 1572872 | tf_op jit(solution)/shard_map/ppermute | solution.py:406
  30.7 5.6 %collective-permute-start.10 = (bf16[128,1024]{1,0:T(8,128)(2,1)}, bf16[128,1024]{1,0:T(8,128)(2,1)S(1)}, u32[]{:S(2)}, u32[]{:S(2)}) collective-permute-start(bf16[128,1024]{1,0:T(8,128)(2,1)} %get-tuple-element.210), channel_id=1, source_target_pairs={{0,1},{1,0},{2,3},{3,2},{4,5},{5,4},{6,7},{7,6},{8,9},{9,8},{10,11... | collective-permute-start | bytes 786440 | tf_op jit(solution)/shard_map/ppermute | solution.py:412
  30.7 5.6 %collective-permute-start.9 = (bf16[128,1024]{1,0:T(8,128)(2,1)}, bf16[128,1024]{1,0:T(8,128)(2,1)}, u32[]{:S(2)}, u32[]{:S(2)}) collective-permute-start(bf16[128,1024]{1,0:T(8,128)(2,1)} %get-tuple-element.211), channel_id=1, source_target_pairs={{0,1},{1,0},{2,3},{3,2},{4,5},{5,4},{6,7},{7,6},{8,9},{9,8},{10,11... | collective-permute-start | bytes 786440 | tf_op jit(solution)/shard_map/ppermute | solution.py:412
  39.8 10.0 %copy-start.1 = (bf16[256,1024]{1,0:T(8,128)(2,1)S(1)}, bf16[256,1024]{1,0:T(8,128)(2,1)}, u32[]{:S(2)}) copy-start(bf16[256,1024]{1,0:T(8,128)(2,1)} %copy-done) | copy-start | bytes 1572868
  39.8 10.0 %copy-start.6 = (bf16[256,1024]{1,0:T(8,128)(2,1)S(1)}, bf16[256,1024]{1,0:T(8,128)(2,1)}, u32[]{:S(2)}) copy-start(bf16[256,1024]{1,0:T(8,128)(2,1)} %copy-done.5) | copy-start | bytes 1572868
  39.8 15.2 %collective-permute-start.12 = (bf16[1024,256]{1,0:T(8,128)(2,1)S(1)}, bf16[1024,256]{1,0:T(8,128)(2,1)S(1)}, u32[]{:S(2)}, u32[]{:S(2)}) collective-permute-start(bf16[1024,256]{1,0:T(8,128)(2,1)S(1)} %broadcast_select_fusion.5), channel_id=1, source_target_pairs={{0,8},{4,12},{8,0},{12,4},{16,24},{20,28},{24,16},{28,20},{1,9},{5... | collective-permute-start | bytes 1572872 | tf_op jit(solution)/shard_map/ppermute | solution.py:407
  44.3 12.2 %collective-permute-start.11 = (bf16[1,2,512,256]{3,2,1,0:T(8,128)(2,1)S(1)}, bf16[1,2,512,256]{3,2,1,0:T(8,128)(2,1)S(1)}, u32[]{:S(2)}, u32[]{:S(2)}) collective-permute-start(bf16[1,2,512,256]{3,2,1,0:T(8,128)(2,1)S(1)} %get-tuple-element.110), channel_id=1, source_target_pairs={{0,4},{4,0},{8,12},{12,8},{16,20},{20,16},{24,28},{28,24},{1,5},{5... | collective-permute-start | bytes 1572872 | tf_op jit(solution)/shard_map/ppermute | solution.py:406
  45.8 10.7 %collective-permute-start.13 = (bf16[1024,256]{1,0:T(8,128)(2,1)}, bf16[1024,256]{1,0:T(8,128)(2,1)S(1)}, u32[]{:S(2)}, u32[]{:S(2)}) collective-permute-start(bf16[1024,256]{1,0:T(8,128)(2,1)} %collective-permute-done.5.refs_0_.refs_1_), channel_id=1, source_target_pairs={{8,16},{16,8},{12,20},{20,12},{9,17},{17,9},{13,21},{21,13},{10,18... | collective-permute-start | bytes 1572872 | tf_op jit(solution)/shard_map/ppermute | solution.py:408
  56.5 13.3 %collective-permute-start.15 = (bf16[1024,256]{1,0:T(8,128)(2,1)S(1)}, bf16[1024,256]{1,0:T(8,128)(2,1)S(1)}, u32[]{:S(2)}, u32[]{:S(2)}) collective-permute-start(bf16[1024,256]{1,0:T(8,128)(2,1)S(1)} %broadcast_select_fusion.4), channel_id=1, source_target_pairs={{0,8},{4,12},{8,0},{12,4},{16,24},{20,28},{24,16},{28,20},{1,9},{5... | collective-permute-start | bytes 1572872 | tf_op jit(solution)/shard_map/ppermute | solution.py:407
  60.3 11.0 %collective-permute-start.14 = (bf16[1,2,512,256]{3,2,1,0:T(8,128)(2,1)S(1)}, bf16[1,2,512,256]{3,2,1,0:T(8,128)(2,1)S(1)}, u32[]{:S(2)}, u32[]{:S(2)}) collective-permute-start(bf16[1,2,512,256]{3,2,1,0:T(8,128)(2,1)S(1)} %get-tuple-element.123), channel_id=1, source_target_pairs={{0,4},{4,0},{8,12},{12,8},{16,20},{20,16},{24,28},{28,24},{1,5},{5... | collective-permute-start | bytes 1572872 | tf_op jit(solution)/shard_map/ppermute | solution.py:406
  60.8 10.5 %collective-permute-start.16 = (bf16[1024,256]{1,0:T(8,128)(2,1)S(1)}, bf16[1024,256]{1,0:T(8,128)(2,1)S(1)}, u32[]{:S(2)}, u32[]{:S(2)}) collective-permute-start(bf16[1024,256]{1,0:T(8,128)(2,1)S(1)} %collective-permute-done.12.refs_0_.refs_1_), channel_id=1, source_target_pairs={{8,16},{16,8},{12,20},{20,12},{9,17},{17,9},{13,21},{21,13},{10,18... | collective-permute-start | bytes 1572872 | tf_op jit(solution)/shard_map/ppermute | solution.py:408
  61.5 23.9 %collective-permute-start.18 = (bf16[1024,256]{1,0:T(8,128)(2,1)S(1)}, bf16[1024,256]{1,0:T(8,128)(2,1)S(1)}, u32[]{:S(2)}, u32[]{:S(2)}) collective-permute-start(bf16[1024,256]{1,0:T(8,128)(2,1)S(1)} %project.7.refs_0_.refs_6_), channel_id=1, source_target_pairs={{8,16},{16,8},{12,20},{20,12},{9,17},{17,9},{13,21},{21,13},{10,18... | collective-permute-start | bytes 1572872 | tf_op jit(solution)/shard_map/ppermute | solution.py:408
  64.9 14.4 %copy-start.4 = (bf16[256,1024]{1,0:T(8,128)(2,1)S(1)}, bf16[256,1024]{1,0:T(8,128)(2,1)}, u32[]{:S(2)}) copy-start(bf16[256,1024]{1,0:T(8,128)(2,1)} %refs_4_.1) | copy-start | bytes 1572868
  71.4 14.0 %collective-permute-start.17 = (bf16[1024,256]{1,0:T(8,128)(2,1)S(1)}, bf16[1024,256]{1,0:T(8,128)(2,1)S(1)}, u32[]{:S(2)}, u32[]{:S(2)}) collective-permute-start(bf16[1024,256]{1,0:T(8,128)(2,1)S(1)} %broadcast_select_fusion.3), channel_id=1, source_target_pairs={{0,8},{4,12},{8,0},{12,4},{16,24},{20,28},{24,16},{28,20},{1,9},{5... | collective-permute-start | bytes 1572872 | tf_op jit(solution)/shard_map/ppermute | solution.py:407
  77.8 12.0 %collective-permute-start.21 = (bf16[1,2,512,256]{3,2,1,0:T(8,128)(2,1)S(1)}, bf16[1,2,512,256]{3,2,1,0:T(8,128)(2,1)S(1)}, u32[]{:S(2)}, u32[]{:S(2)}) collective-permute-start(bf16[1,2,512,256]{3,2,1,0:T(8,128)(2,1)S(1)} %get-tuple-element.146), channel_id=1, source_target_pairs={{0,4},{4,0},{8,12},{12,8},{16,20},{20,16},{24,28},{28,24},{1,5},{5... | collective-permute-start | bytes 1572872 | tf_op jit(solution)/shard_map/ppermute | solution.py:406
  79.3 16.1 %collective-permute-start.26 = (bf16[256,1024]{1,0:T(8,128)(2,1)S(1)}, bf16[256,1024]{1,0:T(8,128)(2,1)S(1)}, u32[]{:S(2)}, u32[]{:S(2)}) collective-permute-start(bf16[256,1024]{1,0:T(8,128)(2,1)S(1)} %copy-done.4), channel_id=1, source_target_pairs={{0,2},{1,3},{2,0},{3,1},{4,6},{5,7},{6,4},{7,5},{8,10},{9,11},{10,... | collective-permute-start | bytes 1572872 | tf_op jit(solution)/shard_map/ppermute | solution.py:393
  85.5 10.1 %collective-permute-start.20 = (bf16[1024,256]{1,0:T(8,128)(2,1)S(1)}, bf16[1024,256]{1,0:T(8,128)(2,1)S(1)}, u32[]{:S(2)}, u32[]{:S(2)}) collective-permute-start(bf16[1024,256]{1,0:T(8,128)(2,1)S(1)} %add.1011), channel_id=1, source_target_pairs={{8,16},{16,8},{12,20},{20,12},{9,17},{17,9},{13,21},{21,13},{10,18... | collective-permute-start | bytes 1572872 | tf_op jit(solution)/shard_map/ppermute | solution.py:408
  86.3 10.6 %collective-permute-start.19 = (bf16[1024,256]{1,0:T(8,128)(2,1)S(1)}, bf16[1024,256]{1,0:T(8,128)(2,1)S(1)}, u32[]{:S(2)}, u32[]{:S(2)}) collective-permute-start(bf16[1024,256]{1,0:T(8,128)(2,1)S(1)} %broadcast_select_fusion.2), channel_id=1, source_target_pairs={{0,8},{4,12},{8,0},{12,4},{16,24},{20,28},{24,16},{28,20},{1,9},{5... | collective-permute-start | bytes 1572872 | tf_op jit(solution)/shard_map/ppermute | solution.py:407
  89.7 20.0 %collective-permute-start.25 = (bf16[256,1024]{1,0:T(8,128)(2,1)S(1)}, bf16[256,1024]{1,0:T(8,128)(2,1)S(1)}, u32[]{:S(2)}, u32[]{:S(2)}) collective-permute-start(bf16[256,1024]{1,0:T(8,128)(2,1)S(1)} %copy-done.4), channel_id=1, source_target_pairs={{0,1},{1,0},{2,3},{3,2},{4,5},{5,4},{6,7},{7,6},{8,9},{9,8},{10,11... | collective-permute-start | bytes 1572872 | tf_op jit(solution)/shard_map/ppermute | solution.py:393
  89.7 14.3 %collective-permute-start.24 = (bf16[1,2,512,256]{3,2,1,0:T(8,128)(2,1)S(1)}, bf16[1,2,512,256]{3,2,1,0:T(8,128)(2,1)S(1)}, u32[]{:S(2)}, u32[]{:S(2)}) collective-permute-start(bf16[1,2,512,256]{3,2,1,0:T(8,128)(2,1)S(1)} %get-tuple-element.151), channel_id=1, source_target_pairs={{0,4},{4,0},{8,12},{12,8},{16,20},{20,16},{24,28},{28,24},{1,5},{5... | collective-permute-start | bytes 1572872 | tf_op jit(solution)/shard_map/ppermute | solution.py:406
  95.4 14.3 %collective-permute-start.27 = (bf16[256,1024]{1,0:T(8,128)(2,1)S(1)}, bf16[256,1024]{1,0:T(8,128)(2,1)S(1)}, u32[]{:S(2)}, u32[]{:S(2)}) collective-permute-start(bf16[256,1024]{1,0:T(8,128)(2,1)S(1)} %collective-permute-done.26.refs_6_), channel_id=1, source_target_pairs={{0,1},{1,0},{2,3},{3,2},{4,5},{5,4},{6,7},{7,6},{8,9},{9,8},{10,11... | collective-permute-start | bytes 1572872 | tf_op jit(solution)/shard_map/ppermute | solution.py:422
  97.0 12.7 %collective-permute-start.23 = (bf16[1024,256]{1,0:T(8,128)(2,1)S(1)}, bf16[1024,256]{1,0:T(8,128)(2,1)S(1)}, u32[]{:S(2)}, u32[]{:S(2)}) collective-permute-start(bf16[1024,256]{1,0:T(8,128)(2,1)S(1)} %add.1012), channel_id=1, source_target_pairs={{8,16},{16,8},{12,20},{20,12},{9,17},{17,9},{13,21},{21,13},{10,18... | collective-permute-start | bytes 1572872 | tf_op jit(solution)/shard_map/ppermute | solution.py:408
  97.8 13.7 %collective-permute-start.22 = (bf16[1024,256]{1,0:T(8,128)(2,1)S(1)}, bf16[1024,256]{1,0:T(8,128)(2,1)S(1)}, u32[]{:S(2)}, u32[]{:S(2)}) collective-permute-start(bf16[1024,256]{1,0:T(8,128)(2,1)S(1)} %broadcast_select_fusion.1), channel_id=1, source_target_pairs={{0,8},{4,12},{8,0},{12,4},{16,24},{20,28},{24,16},{28,20},{1,9},{5... | collective-permute-start | bytes 1572872 | tf_op jit(solution)/shard_map/ppermute | solution.py:407
  104.1 14.8 %collective-permute-start.30 = (bf16[1,2,512,256]{3,2,1,0:T(8,128)(2,1)S(1)}, bf16[1,2,512,256]{3,2,1,0:T(8,128)(2,1)S(1)}, u32[]{:S(2)}, u32[]{:S(2)}) collective-permute-start(bf16[1,2,512,256]{3,2,1,0:T(8,128)(2,1)S(1)} %get-tuple-element.158), channel_id=1, source_target_pairs={{0,4},{4,0},{8,12},{12,8},{16,20},{20,16},{24,28},{28,24},{1,5},{5... | collective-permute-start | bytes 1572872 | tf_op jit(solution)/shard_map/ppermute | solution.py:406
  111.6 11.3 %collective-permute-start.29 = (bf16[1024,256]{1,0:T(8,128)(2,1)S(1)}, bf16[1024,256]{1,0:T(8,128)(2,1)S(1)}, u32[]{:S(2)}, u32[]{:S(2)}) collective-permute-start(bf16[1024,256]{1,0:T(8,128)(2,1)S(1)} %add.1014), channel_id=1, source_target_pairs={{8,16},{16,8},{12,20},{20,12},{9,17},{17,9},{13,21},{21,13},{10,18... | collective-permute-start | bytes 1572872 | tf_op jit(solution)/shard_map/ppermute | solution.py:408
  112.4 12.2 %collective-permute-start.28 = (bf16[1024,256]{1,0:T(8,128)(2,1)S(1)}, bf16[1024,256]{1,0:T(8,128)(2,1)S(1)}, u32[]{:S(2)}, u32[]{:S(2)}) collective-permute-start(bf16[1024,256]{1,0:T(8,128)(2,1)S(1)} %add_select_fusion.1), channel_id=1, source_target_pairs={{0,8},{4,12},{8,0},{12,4},{16,24},{20,28},{24,16},{28,20},{1,9},{5... | collective-permute-start | bytes 1572872 | tf_op jit(solution)/shard_map/ppermute | solution.py:407
  116.1 16.8 %collective-permute-start.33 = (bf16[1,2,512,256]{3,2,1,0:T(8,128)(2,1)S(1)}, bf16[1,2,512,256]{3,2,1,0:T(8,128)(2,1)S(1)}, u32[]{:S(2)}, u32[]{:S(2)}) collective-permute-start(bf16[1,2,512,256]{3,2,1,0:T(8,128)(2,1)S(1)} %get-tuple-element.162), channel_id=1, source_target_pairs={{0,4},{4,0},{8,12},{12,8},{16,20},{20,16},{24,28},{28,24},{1,5},{5... | collective-permute-start | bytes 1572872 | tf_op jit(solution)/shard_map/ppermute | solution.py:406
  124.7 14.8 %collective-permute-start.32 = (bf16[1024,256]{1,0:T(8,128)(2,1)S(1)}, bf16[1024,256]{1,0:T(8,128)(2,1)S(1)}, u32[]{:S(2)}, u32[]{:S(2)}) collective-permute-start(bf16[1024,256]{1,0:T(8,128)(2,1)S(1)} %get-tuple-element.209), channel_id=1, source_target_pairs={{8,16},{16,8},{12,20},{20,12},{9,17},{17,9},{13,21},{21,13},{10,18... | collective-permute-start | bytes 1572872 | tf_op jit(solution)/shard_map/ppermute | solution.py:408
  125.5 14.0 %collective-permute-start.31 = (bf16[1024,256]{1,0:T(8,128)(2,1)S(1)}, bf16[1024,256]{1,0:T(8,128)(2,1)S(1)}, u32[]{:S(2)}, u32[]{:S(2)}) collective-permute-start(bf16[1024,256]{1,0:T(8,128)(2,1)S(1)} %add_select_fusion), channel_id=1, source_target_pairs={{0,8},{4,12},{8,0},{12,4},{16,24},{20,28},{24,16},{28,20},{1,9},{5... | collective-permute-start | bytes 1572872 | tf_op jit(solution)/shard_map/ppermute | solution.py:407
  131.3 6.5 %collective-permute-start.35 = (bf16[256,256]{1,0:T(8,128)(2,1)S(1)}, bf16[256,256]{1,0:T(8,128)(2,1)S(1)}, u32[]{:S(2)}, u32[]{:S(2)}) collective-permute-start(bf16[256,256]{1,0:T(8,128)(2,1)S(1)} %get-tuple-element.170), channel_id=1, source_target_pairs={{0,2},{1,3},{2,0},{3,1},{4,6},{5,7},{6,4},{7,5},{8,10},{9,11},{10,... | collective-permute-start | bytes 393224 | tf_op jit(solution)/shard_map/ppermute | solution.py:331
  132.9 5.8 %collective-permute-start.36 = (bf16[256,256]{1,0:T(8,128)(2,1)S(1)}, bf16[256,256]{1,0:T(8,128)(2,1)S(1)}, u32[]{:S(2)}, u32[]{:S(2)}) collective-permute-start(bf16[256,256]{1,0:T(8,128)(2,1)S(1)} %get-tuple-element.171), channel_id=1, source_target_pairs={{0,3},{1,2},{2,1},{3,0},{4,7},{5,6},{6,5},{7,4},{8,11},{9,10},{10,... | collective-permute-start | bytes 393224 | tf_op jit(solution)/shard_map/ppermute | solution.py:331
  132.9 5.8 %copy-start.9 = (f32[1024]{0:T(1024)S(1)}, f32[1024]{0:T(1024)}, u32[]{:S(2)}) copy-start(f32[1024]{0:T(1024)} %param.16) | copy-start | bytes 12292
  132.9 5.8 %collective-permute-start.34 = (bf16[256,256]{1,0:T(8,128)(2,1)S(1)}, bf16[256,256]{1,0:T(8,128)(2,1)S(1)}, u32[]{:S(2)}, u32[]{:S(2)}) collective-permute-start(bf16[256,256]{1,0:T(8,128)(2,1)S(1)} %get-tuple-element.169), channel_id=1, source_target_pairs={{0,1},{1,0},{2,3},{3,2},{4,5},{5,4},{6,7},{7,6},{8,9},{9,8},{10,11... | collective-permute-start | bytes 393224 | tf_op jit(solution)/shard_map/ppermute | solution.py:331
  140.6 6.4 %collective-permute-start.38 = (bf16[256,256]{1,0:T(8,128)(2,1)S(1)}, bf16[256,256]{1,0:T(8,128)(2,1)S(1)}, u32[]{:S(2)}, u32[]{:S(2)}) collective-permute-start(bf16[256,256]{1,0:T(8,128)(2,1)S(1)} %get-tuple-element.186), channel_id=1, source_target_pairs={{0,2},{1,3},{2,0},{3,1},{4,6},{5,7},{6,4},{7,5},{8,10},{9,11},{10,... | collective-permute-start | bytes 393224 | tf_op jit(solution)/shard_map/ppermute | solution.py:331
  141.4 7.2 %collective-permute-start.39 = (bf16[256,256]{1,0:T(8,128)(2,1)S(1)}, bf16[256,256]{1,0:T(8,128)(2,1)S(1)}, u32[]{:S(2)}, u32[]{:S(2)}) collective-permute-start(bf16[256,256]{1,0:T(8,128)(2,1)S(1)} %get-tuple-element.187), channel_id=1, source_target_pairs={{0,3},{1,2},{2,1},{3,0},{4,7},{5,6},{6,5},{7,4},{8,11},{9,10},{10,... | collective-permute-start | bytes 393224 | tf_op jit(solution)/shard_map/ppermute | solution.py:331
  143.4 5.2 %collective-permute-start.37 = (bf16[256,256]{1,0:T(8,128)(2,1)S(1)}, bf16[256,256]{1,0:T(8,128)(2,1)S(1)}, u32[]{:S(2)}, u32[]{:S(2)}) collective-permute-start(bf16[256,256]{1,0:T(8,128)(2,1)S(1)} %get-tuple-element.185), channel_id=1, source_target_pairs={{0,1},{1,0},{2,3},{3,2},{4,5},{5,4},{6,7},{7,6},{8,9},{9,8},{10,11... | collective-permute-start | bytes 393224 | tf_op jit(solution)/shard_map/ppermute | solution.py:331
  (5 other events, 15.0 us)
where the time goes:
time: 151 us
  starting transfers between devices  59.3 us (39%)
  Pallas kernels  54.2 us (36%)
  waiting for transfers between devices  27.6 us (18%)
  local copies, waits for them, and re-layouts  6.73 us (4%)
  other arithmetic  1.71 us (1%)
    pallas_call x20, Pallas kernels, local_call(): pl.pallas_call(kernel, in_specs=[pl.BlockSpec(memory_space=places.get(i,...  54.2 us
    ppermute x8, starting transfers between devices, local(): outer.append(exchange_outer(to_outer))  32.1 us
    ppermute x7, starting transfers between devices, local(): held, page = (page, swap_page(sending) if step < 7 else page)  8.62 us
    ppermute x7, waiting for transfers between devices, local(): held, page = (page, swap_page(sending) if step < 7 else page)  8.56 us
    ppermute x8, waiting for transfers between devices, local(): outer.append(exchange_outer(to_outer))  7.9 us
    ppermute x8, starting transfers between devices, local(): inner.append(exchange_inner(to_inner))  6.29 us
    ppermute x6, waiting for transfers between devices, spread(): return [near[0], swap_core(near[1]), swap_chip(far[0]), swap_both(far[1])]  5.48 us
    ppermute x6, starting transfers between devices, spread(): return [near[0], swap_core(near[1]), swap_chip(far[0]), swap_both(far[1])]  4.48 us
  transfers between devices with their start and end apart: 40, of which 16 were waited for; matrix products, arithmetic and copies ran while one was open for 4% of the time, Pallas kernels for 34%

commit v1 on v0

--- a/solution.py
+++ b/solution.py
@@ -310,7 +310,7 @@
     swap_both = swap("cand", 3)
     swap_page = swap("cache", 1)
 
-    states = jnp.moveaxis(cand_states, 1, 0)
+    states = [cand_states[:, member] for member in range(users_here)]
     in_matrix = in_proj.reshape(width, 4 * head_width)
     table = bias_rows(recency_bias, cache_count * events // BLOCK)
     first_bias = recency_bias[:, 0]
@@ -389,7 +389,7 @@
             if step == 3:
                 to_outer, to_inner = either(totals[2], inner[2]), query_b
                 queries = [outer[2], outer[0]]
-                to_outer, out_mine = tied(to_outer, out_proj)
+                to_outer, to_inner, out_mine = tied(to_outer, to_inner, out_proj)
                 out_across, out_near = swap_chip(out_mine), swap_core(out_mine)
             if step == 4:
                 to_outer, to_inner = either(totals[3], inner[3]), outer[3] + totals[1]

time: 151 us -> 153 us (1.013)
  local copies, waits for them, and re-layouts: 6.73 us -> 8.91 us
  waiting for transfers between devices: 27.6 us -> 25.9 us
  Pallas kernels: 54.2 us -> 55.8 us
    slice x0 -> x1, local copies, waits for them, and re-layouts: none -> 3.41 us  [local(): states = [cand_states[:, member] for member in range(users_here)]]
    ppermute x8, waiting for transfers between devices: 7.9 us -> 5.92 us  [local(): outer.append(exchange_outer(to_outer))]
    pallas_call x20, Pallas kernels: 54.2 us -> 55.8 us  [local_call(): pl.pallas_call(kernel, in_specs=[pl.BlockSpec(memory_space=places.get(i,...]
    unnamed x28 -> x29, local copies, waits for them, and re-layouts: 4.45 us -> 3.29 us
  transfers between devices with their start and end apart: 40 -> 40, of which waited for: 16 -> 16; matrix products, arithmetic and copies ran while one was open for 4% -> 4% of each run, Pallas kernels for 34% -> 35%
where the time goes in v1:
time: 153 us; the launch traced here: 152 us
  starting transfers between devices  58.6 us (38%)
  Pallas kernels  55.8 us (36%)
  waiting for transfers between devices  25.9 us (17%)
  local copies, waits for them, and re-layouts  8.91 us (6%)
  other arithmetic  1.71 us (1%)
    pallas_call x20, Pallas kernels, local_call(): pl.pallas_call(kernel, in_specs=[pl.BlockSpec(memory_space=places.get(i,...  55.8 us
    ppermute x8, starting transfers between devices, local(): outer.append(exchange_outer(to_outer))  31.4 us
    ppermute x7, waiting for transfers between devices, local(): held, page = (page, swap_page(sending) if step < 7 else page)  9.19 us
    ppermute x7, starting transfers between devices, local(): held, page = (page, swap_page(sending) if step < 7 else page)  8.68 us
    ppermute x8, starting transfers between devices, local(): inner.append(exchange_inner(to_inner))  6.28 us
    ppermute x8, waiting for transfers between devices, local(): outer.append(exchange_outer(to_outer))  5.92 us
    ppermute x6, waiting for transfers between devices, spread(): return [near[0], swap_core(near[1]), swap_chip(far[0]), swap_both(far[1])]  5.44 us
    ppermute x6, starting transfers between devices, spread(): return [near[0], swap_core(near[1]), swap_chip(far[0]), swap_both(far[1])]  4.48 us
  transfers between devices with their start and end apart: 40, of which 16 were waited for; matrix products, arithmetic and copies ran while one was open for 4% of the time, Pallas kernels for 35%

profile of v1, /device:TPU:0, one launch (start us, length us, event | category | flops | bytes accessed | tf_op | source)
XLA Modules:
  0.0 152.1 jit_solution(17267676499438669207)
XLA Ops:
  0.6 3.4 %fusion.17 = (bf16[256,1,1024]{2,1,0:T(2,128)(2,1)S(1)}, bf16[256,1,1024]{2,1,0:T(2,128)(2,1)S(1)}) fusion(bf16[256,2,1024]{2,1,0:T(2,128)(2,1)} %param.9), kind=kLoop, calls=%fused_computation.77 | loop fusion | bytes 2097152 | tf_op jit(solution)/shard_map/slice | solution.py:313
  4.8 2.6 %collective-permute-start = (bf16[256,1024]{1,0:T(8,128)(2,1)S(1)}, bf16[256,1024]{1,0:T(8,128)(2,1)}, u32[]{:S(2)}, u32[]{:S(2)}) collective-permute-start(bf16[256,1024]{1,0:T(8,128)(2,1)S(1)} %bitcast.40), channel_id=1, source_target_pairs={{0,2},{1,3},{2,0},{3,1},{4,6},{5,7},{6,4},{7,5},{8,10},{9,11},{10,... | collective-permute-start | bytes 1572872 | tf_op jit(solution)/shard_map/ppermute | solution.py:366
  8.6 2.9 %pages.1 = (bf16[1,2,512,256]{3,2,1,0:T(8,128)(2,1)}, bf16[1,2,512,256]{3,2,1,0:T(8,128)(2,1)}) custom-call(s32[2]{0:T(128)S(1)} %bitcast.46, bf16[1,16,2,512,256]{4,3,2,1,0:T(8,128)(2,1)} %history.17), custom_call_target="tpu_custom_call" | custom-call | flops 1 | bytes 1 | tf_op jit(solution)/shard_map/pages/pallas_call | solution.py:25
  11.5 1.6 %collective-permute-start.7 = (bf16[1,2,512,256]{3,2,1,0:T(8,128)(2,1)}, bf16[1,2,512,256]{3,2,1,0:T(8,128)(2,1)}, u32[]{:S(2)}, u32[]{:S(2)}) collective-permute-start(bf16[1,2,512,256]{3,2,1,0:T(8,128)(2,1)} %get-tuple-element.107), channel_id=1, source_target_pairs={{0,4},{4,0},{8,12},{12,8},{16,20},{20,16},{24,28},{28,24},{1,5},{5... | collective-permute-start | bytes 1572872 | tf_op jit(solution)/shard_map/ppermute | solution.py:370
  13.1 2.1 %copy.19 = bf16[128,8,4,256]{3,1,2,0:T(8,128)(2,1)S(1)} copy(bf16[128,8,4,256]{3,2,1,0:T(4,128)(2,1)} %bitcast.48) | data formatting | bytes 4194304
  16.5 2.2 %project.5 = (bf16[512,256]{1,0:T(8,128)(2,1)S(1)}, bf16[512,256]{1,0:T(8,128)(2,1)S(1)}) custom-call(bf16[1024,1024]{1,0:T(8,128)(2,1)S(1)} %bitcast.29, bf16[256,1024]{1,0:T(8,128)(2,1)S(1)} %bitcast.41, bf16[256,1024]{1,0:T(8,128)(2,1)} %collective-permute-done.1.refs_1_, bf16[256,1024]{1,0:T(8,128)(2,1)S(1)} %bitcast.36, ...), custom_call_target="tpu_custom_call" | custom-call | flops 1 | bytes 1 | tf_op jit(solution)/shard_map/project/pallas_call | solution.py:25
  18.6 1.6 %collective-permute-done.refs_0_.refs_2_ = bf16[256,1024]{1,0:T(8,128)(2,1)} collective-permute-done((bf16[256,1024]{1,0:T(8,128)(2,1)S(1)}, bf16[256,1024]{1,0:T(8,128)(2,1)}, u32[]{:S(2)}, u32[]{:S(2)}) %collective-permute-start) | collective-permute-done | bytes 524320 | tf_op jit(solution)/shard_map/ppermute | solution.py:366
  20.4 1.9 %collective-permute-done.3.refs_1_.refs_3_ = bf16[256,1024]{1,0:T(8,128)(2,1)S(1)} collective-permute-done((bf16[256,1024]{1,0:T(8,128)(2,1)}, bf16[256,1024]{1,0:T(8,128)(2,1)S(1)}, u32[]{:S(2)}, u32[]{:S(2)}) %collective-permute-start.3) | collective-permute-done | bytes 524320 | tf_op jit(solution)/shard_map/ppermute | solution.py:375
  22.3 1.8 %project.6.refs_0_.refs_6_ = bf16[1024,256]{1,0:T(8,128)(2,1)S(1)} custom-call(bf16[1024,1024]{1,0:T(8,128)(2,1)S(1)} %bitcast.30, bf16[512,256]{1,0:T(8,128)(2,1)S(1)} %get-tuple-element.101.ahead, bf16[256,1024]{1,0:T(8,128)(2,1)} %collective-permute-done.refs_0_.refs_2_, bf16[256,1024]{1,0:T(8,128)(2,1)S(1)} %collective-permute-done.3.refs_1_.refs_3_), custom_call_target="tpu_custom_call" | custom-call | flops 1 | bytes 1 | tf_op jit(solution)/shard_map/project/pallas_call | solution.py:25
  24.1 2.1 %collective-permute-start.5 = (bf16[1024,256]{1,0:T(8,128)(2,1)S(1)}, bf16[1024,256]{1,0:T(8,128)(2,1)}, u32[]{:S(2)}, u32[]{:S(2)}) collective-permute-start(bf16[1024,256]{1,0:T(8,128)(2,1)S(1)} %project.6.refs_0_.refs_6_), channel_id=1, source_target_pairs={{0,8},{4,12},{8,0},{12,4},{16,24},{20,28},{24,16},{28,20},{1,9},{5... | collective-permute-start | bytes 1572872 | tf_op jit(solution)/shard_map/ppermute | solution.py:407
  26.2 1.5 collective-permute-start.6
  27.7 1.5 %collective-permute-start.4 = (bf16[1,2,512,256]{3,2,1,0:T(8,128)(2,1)}, bf16[1,2,512,256]{3,2,1,0:T(8,128)(2,1)}, u32[]{:S(2)}, u32[]{:S(2)}) collective-permute-start(bf16[1,2,512,256]{3,2,1,0:T(8,128)(2,1)} %get-tuple-element.104), channel_id=1, source_target_pairs={{0,4},{4,0},{8,12},{12,8},{16,20},{20,16},{24,28},{28,24},{1,5},{5... | collective-permute-start | bytes 1572872 | tf_op jit(solution)/shard_map/ppermute | solution.py:406
  29.2 1.9 %collective-permute-done.8.refs_0_.refs_2_ = bf16[256,1024]{1,0:T(8,128)(2,1)S(1)} collective-permute-done((bf16[256,1024]{1,0:T(8,128)(2,1)S(1)}, bf16[256,1024]{1,0:T(8,128)(2,1)S(1)}, u32[]{:S(2)}, u32[]{:S(2)}) %collective-permute-start.8) | collective-permute-done | bytes 524320 | tf_op jit(solution)/shard_map/ppermute | solution.py:368
  33.7 4.7 %attend.8 = (bf16[1024,256]{1,0:T(8,128)(2,1)S(1)}, bf16[1,2,512,256]{3,2,1,0:T(8,128)(2,1)S(1)}) custom-call(s32[48]{0:T(128)S(1)} %reshape.389.picks, bf16[1,16,2,512,256]{4,3,2,1,0:T(8,128)(2,1)} %history.17, bf16[1,2,512,256]{3,2,1,0:T(8,128)(2,1)} %collective-permute-done.7.other, f32[2,33,128]{2,1,0:T(8,128)S(1)} %concatenate.8.table, ...), custom_call_target="tpu_custom_call" | custom-call | flops 1 | bytes 1 | tf_op jit(solution)/shard_map/attend/pallas_call | solution.py:25
  38.4 1.5 %project.7.refs_0_.refs_6_ = bf16[1024,256]{1,0:T(8,128)(2,1)S(1)} custom-call(bf16[1024,1024]{1,0:T(8,128)(2,1)S(1)} %bitcast.31, bf16[512,256]{1,0:T(8,128)(2,1)S(1)} %copy-done.8, bf16[256,1024]{1,0:T(8,128)(2,1)S(1)} %copy-done.3, bf16[128,1024]{1,0:T(8,128)(2,1)} %collective-permute-done.9.refs_1_.refs_3_, ...), custom_call_target="tpu_custom_call" | custom-call | flops 1 | bytes 1 | tf_op jit(solution)/shard_map/project/pallas_call | solution.py:25
  39.9 1.8 %collective-permute-done.4.other = bf16[1,2,512,256]{3,2,1,0:T(8,128)(2,1)} collective-permute-done((bf16[1,2,512,256]{3,2,1,0:T(8,128)(2,1)}, bf16[1,2,512,256]{3,2,1,0:T(8,128)(2,1)}, u32[]{:S(2)}, u32[]{:S(2)}) %collective-permute-start.4) | collective-permute-done | bytes 524320 | tf_op jit(solution)/shard_map/ppermute | solution.py:406
  41.8 4.5 %collective-permute-start.12 = (bf16[1024,256]{1,0:T(8,128)(2,1)S(1)}, bf16[1024,256]{1,0:T(8,128)(2,1)S(1)}, u32[]{:S(2)}, u32[]{:S(2)}) collective-permute-start(bf16[1024,256]{1,0:T(8,128)(2,1)S(1)} %broadcast_select_fusion.5), channel_id=1, source_target_pairs={{0,8},{4,12},{8,0},{12,4},{16,24},{20,28},{24,16},{28,20},{1,9},{5... | collective-permute-start | bytes 1572872 | tf_op jit(solution)/shard_map/ppermute | solution.py:407
  46.3 1.5 collective-permute-start.11
  48.5 3.3 %attend.9 = (bf16[1024,256]{1,0:T(8,128)(2,1)S(1)}, bf16[1,2,512,256]{3,2,1,0:T(8,128)(2,1)S(1)}) custom-call(s32[48]{0:T(128)S(1)} %reshape.389.picks, bf16[1,16,2,512,256]{4,3,2,1,0:T(8,128)(2,1)} %history.17, bf16[1,2,512,256]{3,2,1,0:T(8,128)(2,1)} %collective-permute-done.4.other, f32[2,33,128]{2,1,0:T(8,128)S(1)} %concatenate.8.table, ...), custom_call_target="tpu_custom_call" | custom-call | flops 1 | bytes 1 | tf_op jit(solution)/shard_map/attend/pallas_call | solution.py:25
  51.8 3.4 %project.8 = (bf16[1024,256]{1,0:T(8,128)(2,1)S(1)}, bf16[1024,256]{1,0:T(8,128)(2,1)S(1)}, bf16[1024,256]{1,0:T(8,128)(2,1)S(1)}) custom-call(bf16[1024,1024]{1,0:T(8,128)(2,1)S(1)} %bitcast.32, bf16[256,1024]{1,0:T(8,128)(2,1)S(1)} %bitcast.42, bf16[256,1024]{1,0:T(8,128)(2,1)} %collective-permute-done.1.refs_1_, ...), custom_call_target="tpu_custom_call" | custom-call | flops 1 | bytes 1 | tf_op jit(solution)/shard_map/project/pallas_call | solution.py:25
  55.3 1.8 %collective-permute-done.12.refs_0_.refs_1_ = bf16[1024,256]{1,0:T(8,128)(2,1)S(1)} collective-permute-done((bf16[1024,256]{1,0:T(8,128)(2,1)S(1)}, bf16[1024,256]{1,0:T(8,128)(2,1)S(1)}, u32[]{:S(2)}, u32[]{:S(2)}) %collective-permute-start.12) | collective-permute-done | bytes 524320 | tf_op jit(solution)/shard_map/ppermute | solution.py:407
  57.0 1.5 collective-permute-done.11.other
  58.6 3.8 %collective-permute-start.15 = (bf16[1024,256]{1,0:T(8,128)(2,1)S(1)}, bf16[1024,256]{1,0:T(8,128)(2,1)S(1)}, u32[]{:S(2)}, u32[]{:S(2)}) collective-permute-start(bf16[1024,256]{1,0:T(8,128)(2,1)S(1)} %broadcast_select_fusion.4), channel_id=1, source_target_pairs={{0,8},{4,12},{8,0},{12,4},{16,24},{20,28},{24,16},{28,20},{1,9},{5... | collective-permute-start | bytes 1572872 | tf_op jit(solution)/shard_map/ppermute | solution.py:407
  63.5 4.3 %attend.10 = (bf16[1024,256]{1,0:T(8,128)(2,1)S(1)}, bf16[1,2,512,256]{3,2,1,0:T(8,128)(2,1)S(1)}) custom-call(s32[48]{0:T(128)S(1)} %reshape.389.picks, bf16[1,16,2,512,256]{4,3,2,1,0:T(8,128)(2,1)} %history.17, bf16[1,2,512,256]{3,2,1,0:T(8,128)(2,1)S(1)} %collective-permute-done.11.other, f32[2,33,128]{2,1,0:T(8,128)S(1)} %concatenate.8.table, ...), custom_call_target="tpu_custom_call" | custom-call | flops 1 | bytes 1 | tf_op jit(solution)/shard_map/attend/pallas_call | solution.py:25
  67.8 3.5 %project.9 = (bf16[1024,256]{1,0:T(8,128)(2,1)S(1)}, bf16[1024,256]{1,0:T(8,128)(2,1)S(1)}, bf16[1024,256]{1,0:T(8,128)(2,1)S(1)}) custom-call(bf16[1024,1024]{1,0:T(8,128)(2,1)S(1)} %bitcast.33, bf16[256,1024]{1,0:T(8,128)(2,1)S(1)} %bitcast.37, bf16[256,1024]{1,0:T(8,128)(2,1)} %collective-permute-done.2.refs_3_.refs_1_, bf16[256,1024]{1,0:T(8,128)(2,1)S(1)} %copy-done.3, ...), custom_call_target="tpu_custom_call" | custom-call | flops 1 | bytes 1 | tf_op jit(solution)/shard_map/project/pallas_call | solution.py:25
  71.9 1.5 collective-permute-done.14.other
  73.4 2.5 %collective-permute-start.17 = (bf16[1024,256]{1,0:T(8,128)(2,1)S(1)}, bf16[1024,256]{1,0:T(8,128)(2,1)S(1)}, u32[]{:S(2)}, u32[]{:S(2)}) collective-permute-start(bf16[1024,256]{1,0:T(8,128)(2,1)S(1)} %broadcast_select_fusion.3), channel_id=1, source_target_pairs={{0,8},{4,12},{8,0},{12,4},{16,24},{20,28},{24,16},{28,20},{1,9},{5... | collective-permute-start | bytes 1572872 | tf_op jit(solution)/shard_map/ppermute | solution.py:407
  76.6 1.6 %collective-permute-start.21 = (bf16[1,2,512,256]{3,2,1,0:T(8,128)(2,1)S(1)}, bf16[1,2,512,256]{3,2,1,0:T(8,128)(2,1)S(1)}, u32[]{:S(2)}, u32[]{:S(2)}) collective-permute-start(bf16[1,2,512,256]{3,2,1,0:T(8,128)(2,1)S(1)} %get-tuple-element.148), channel_id=1, source_target_pairs={{0,4},{4,0},{8,12},{12,8},{16,20},{20,16},{24,28},{28,24},{1,5},{5... | collective-permute-start | bytes 1572872 | tf_op jit(solution)/shard_map/ppermute | solution.py:406
  78.2 1.5 collective-permute-start.26
  79.7 4.6 %attend.11 = (bf16[1024,256]{1,0:T(8,128)(2,1)S(1)}, bf16[1,2,512,256]{3,2,1,0:T(8,128)(2,1)S(1)}) custom-call(s32[48]{0:T(128)S(1)} %reshape.389.picks, bf16[1,16,2,512,256]{4,3,2,1,0:T(8,128)(2,1)} %history.17, bf16[1,2,512,256]{3,2,1,0:T(8,128)(2,1)S(1)} %collective-permute-done.14.other, f32[2,33,128]{2,1,0:T(8,128)S(1)} %concatenate.8.table, ...), custom_call_target="tpu_custom_call" | custom-call | flops 1 | bytes 1 | tf_op jit(solution)/shard_map/attend/pallas_call | solution.py:25
  85.2 6.1 %collective-permute-start.19 = (bf16[1024,256]{1,0:T(8,128)(2,1)S(1)}, bf16[1024,256]{1,0:T(8,128)(2,1)S(1)}, u32[]{:S(2)}, u32[]{:S(2)}) collective-permute-start(bf16[1024,256]{1,0:T(8,128)(2,1)S(1)} %broadcast_select_fusion.2), channel_id=1, source_target_pairs={{0,8},{4,12},{8,0},{12,4},{16,24},{20,28},{24,16},{28,20},{1,9},{5... | collective-permute-start | bytes 1572872 | tf_op jit(solution)/shard_map/ppermute | solution.py:407
  91.3 1.5 collective-permute-start.24
  92.9 4.1 %attend.12 = (bf16[1024,256]{1,0:T(8,128)(2,1)S(1)}, bf16[1,2,512,256]{3,2,1,0:T(8,128)(2,1)S(1)}) custom-call(s32[48]{0:T(128)S(1)} %reshape.389.picks, bf16[1,16,2,512,256]{4,3,2,1,0:T(8,128)(2,1)} %history.17, bf16[1,2,512,256]{3,2,1,0:T(8,128)(2,1)S(1)} %collective-permute-done.21.other, f32[2,33,128]{2,1,0:T(8,128)S(1)} %concatenate.8.table, ...), custom_call_target="tpu_custom_call" | custom-call | flops 1 | bytes 1 | tf_op jit(solution)/shard_map/attend/pallas_call | solution.py:25
  97.3 1.5 %collective-permute-done.19.refs_0_ = bf16[1024,256]{1,0:T(8,128)(2,1)S(1)} collective-permute-done((bf16[1024,256]{1,0:T(8,128)(2,1)S(1)}, bf16[1024,256]{1,0:T(8,128)(2,1)S(1)}, u32[]{:S(2)}, u32[]{:S(2)}) %collective-permute-start.19) | collective-permute-done | bytes 524320 | tf_op jit(solution)/shard_map/ppermute | solution.py:407
  99.7 3.8 %collective-permute-start.22 = (bf16[1024,256]{1,0:T(8,128)(2,1)S(1)}, bf16[1024,256]{1,0:T(8,128)(2,1)S(1)}, u32[]{:S(2)}, u32[]{:S(2)}) collective-permute-start(bf16[1024,256]{1,0:T(8,128)(2,1)S(1)} %broadcast_select_fusion.1), channel_id=1, source_target_pairs={{0,8},{4,12},{8,0},{12,4},{16,24},{20,28},{24,16},{28,20},{1,9},{5... | collective-permute-start | bytes 1572872 | tf_op jit(solution)/shard_map/ppermute | solution.py:407
  103.5 2.2 %collective-permute-done.24.other = bf16[1,2,512,256]{3,2,1,0:T(8,128)(2,1)S(1)} collective-permute-done((bf16[1,2,512,256]{3,2,1,0:T(8,128)(2,1)S(1)}, bf16[1,2,512,256]{3,2,1,0:T(8,128)(2,1)S(1)}, u32[]{:S(2)}, u32[]{:S(2)}) %collective-permute-start.24) | collective-permute-done | bytes 524320 | tf_op jit(solution)/shard_map/ppermute | solution.py:406
  105.7 1.5 collective-permute-start.30
  107.2 4.1 %attend.13 = (bf16[1024,256]{1,0:T(8,128)(2,1)S(1)}, bf16[1,2,512,256]{3,2,1,0:T(8,128)(2,1)S(1)}) custom-call(s32[48]{0:T(128)S(1)} %reshape.389.picks, bf16[1,16,2,512,256]{4,3,2,1,0:T(8,128)(2,1)} %history.17, bf16[1,2,512,256]{3,2,1,0:T(8,128)(2,1)S(1)} %collective-permute-done.24.other, f32[2,33,128]{2,1,0:T(8,128)S(1)} %concatenate.8.table, ...), custom_call_target="tpu_custom_call" | custom-call | flops 1 | bytes 1 | tf_op jit(solution)/shard_map/attend/pallas_call | solution.py:25
  113.3 4.4 %collective-permute-start.28 = (bf16[1024,256]{1,0:T(8,128)(2,1)S(1)}, bf16[1024,256]{1,0:T(8,128)(2,1)S(1)}, u32[]{:S(2)}, u32[]{:S(2)}) collective-permute-start(bf16[1024,256]{1,0:T(8,128)(2,1)S(1)} %add_select_fusion.1), channel_id=1, source_target_pairs={{0,8},{4,12},{8,0},{12,4},{16,24},{20,28},{24,16},{28,20},{1,9},{5... | collective-permute-start | bytes 1572872 | tf_op jit(solution)/shard_map/ppermute | solution.py:407
  118.2 2.3 %collective-permute-done.30.other = bf16[1,2,512,256]{3,2,1,0:T(8,128)(2,1)S(1)} collective-permute-done((bf16[1,2,512,256]{3,2,1,0:T(8,128)(2,1)S(1)}, bf16[1,2,512,256]{3,2,1,0:T(8,128)(2,1)S(1)}, u32[]{:S(2)}, u32[]{:S(2)}) %collective-permute-start.30) | collective-permute-done | bytes 524320 | tf_op jit(solution)/shard_map/ppermute | solution.py:406
  120.5 4.1 %attend.14 = bf16[1024,256]{1,0:T(8,128)(2,1)S(1)} custom-call(s32[48]{0:T(128)S(1)} %reshape.389.picks, bf16[1,16,2,512,256]{4,3,2,1,0:T(8,128)(2,1)} %history.17, bf16[1,2,512,256]{3,2,1,0:T(8,128)(2,1)S(1)} %collective-permute-done.30.other, f32[2,33,128]{2,1,0:T(8,128)S(1)} %concatenate.8.table, bf16[1024,256]{1,0:T(8,128)(2,1)S(1)} %collective-permute-done.22.refs_0_, ...), custom_call_target="tpu_custom_call" | custom-call | flops 1 | bytes 1 | tf_op jit(solution)/shard_map/attend/pallas_call | solution.py:25
  126.5 4.3 %collective-permute-start.31 = (bf16[1024,256]{1,0:T(8,128)(2,1)S(1)}, bf16[1024,256]{1,0:T(8,128)(2,1)S(1)}, u32[]{:S(2)}, u32[]{:S(2)}) collective-permute-start(bf16[1024,256]{1,0:T(8,128)(2,1)S(1)} %add_select_fusion), channel_id=1, source_target_pairs={{0,8},{4,12},{8,0},{12,4},{16,24},{20,28},{24,16},{28,20},{1,9},{5... | collective-permute-start | bytes 1572872 | tf_op jit(solution)/shard_map/ppermute | solution.py:407
  132.9 1.6 %collective-permute-start.35 = (bf16[256,256]{1,0:T(8,128)(2,1)S(1)}, bf16[256,256]{1,0:T(8,128)(2,1)S(1)}, u32[]{:S(2)}, u32[]{:S(2)}) collective-permute-start(bf16[256,256]{1,0:T(8,128)(2,1)S(1)} %get-tuple-element.172), channel_id=1, source_target_pairs={{0,2},{1,3},{2,0},{3,1},{4,6},{5,7},{6,4},{7,5},{8,10},{9,11},{10,... | collective-permute-start | bytes 393224 | tf_op jit(solution)/shard_map/ppermute | solution.py:331
  135.1 4.3 %attend.15.refs_0_ = bf16[1024,256]{1,0:T(8,128)(2,1)S(1)} custom-call(s32[48]{0:T(128)S(1)} %reshape.389.picks, bf16[1,16,2,512,256]{4,3,2,1,0:T(8,128)(2,1)} %history.17, bf16[1,2,512,256]{3,2,1,0:T(8,128)(2,1)S(1)} %collective-permute-done.33.other, f32[2,33,128]{2,1,0:T(8,128)S(1)} %concatenate.8.table, bf16[1024,256]{1,0:T(8,128)(2,1)S(1)} %project.7.refs_0_.refs_6_), custom_call_target="tpu_custom_call" | custom-call | flops 1 | bytes 1 | tf_op jit(solution)/shard_map/attend/pallas_call | solution.py:25
  141.1 1.1 finish.7
  145.5 3.0 %collective-permute-done.38.refs_2_ = bf16[256,256]{1,0:T(8,128)(2,1)S(1)} collective-permute-done((bf16[256,256]{1,0:T(8,128)(2,1)S(1)}, bf16[256,256]{1,0:T(8,128)(2,1)S(1)}, u32[]{:S(2)}, u32[]{:S(2)}) %collective-permute-start.38) | collective-permute-done | bytes 131104 | tf_op jit(solution)/shard_map/ppermute | solution.py:331
  148.6 1.5 %collective-permute-done.39.refs_3_ = bf16[256,256]{1,0:T(8,128)(2,1)S(1)} collective-permute-done((bf16[256,256]{1,0:T(8,128)(2,1)S(1)}, bf16[256,256]{1,0:T(8,128)(2,1)S(1)}, u32[]{:S(2)}, u32[]{:S(2)}) %collective-permute-start.39) | collective-permute-done | bytes 131104 | tf_op jit(solution)/shard_map/ppermute | solution.py:331
  150.1 2.0 %combine.3 = (bf16[256,2,1024]{2,1,0:T(2,128)(2,1)}, f32[2,256]{1,0:T(2,128)}) custom-call(bf16[256,1024]{1,0:T(8,128)(2,1)S(1)} %bitcast.38, f32[1,1024]{1,0:T(1,128)S(1)} %bitcast.45, bf16[256,256]{1,0:T(8,128)(2,1)S(1)} %get-tuple-element.186.refs_0_, bf16[256,256]{1,0:T(8,128)(2,1)S(1)} %collective-permute-done.37.refs_1_, ...), custom_call_target="tpu_custom_call" | custom-call | flops 1 | bytes 1 | tf_op jit(solution)/shard_map/combine/pallas_call | solution.py:25
  (110 shorter events, 23.6 us)
Async XLA Ops:
  4.2 12.2 %copy-start = (bf16[256,1,1024]{2,0,1:T(8,128)(2,1)}, bf16[256,1,1024]{2,0,1:T(8,128)(2,1)S(1)}, u32[]{:S(2)}) copy-start(bf16[256,1,1024]{2,0,1:T(8,128)(2,1)S(1)} %copy.22) | copy-start | bytes 1572868
  4.2 11.6 %collective-permute-start.1 = (bf16[256,1024]{1,0:T(8,128)(2,1)S(1)}, bf16[256,1024]{1,0:T(8,128)(2,1)}, u32[]{:S(2)}, u32[]{:S(2)}) collective-permute-start(bf16[256,1024]{1,0:T(8,128)(2,1)S(1)} %bitcast.39), channel_id=1, source_target_pairs={{0,1},{1,0},{2,3},{3,2},{4,5},{5,4},{6,7},{7,6},{8,9},{9,8},{10,11... | collective-permute-start | bytes 1572872 | tf_op jit(solution)/shard_map/ppermute | solution.py:366
  4.8 15.4 %collective-permute-start = (bf16[256,1024]{1,0:T(8,128)(2,1)S(1)}, bf16[256,1024]{1,0:T(8,128)(2,1)}, u32[]{:S(2)}, u32[]{:S(2)}) collective-permute-start(bf16[256,1024]{1,0:T(8,128)(2,1)S(1)} %bitcast.40), channel_id=1, source_target_pairs={{0,2},{1,3},{2,0},{3,1},{4,6},{5,7},{6,4},{7,5},{8,10},{9,11},{10,... | collective-permute-start | bytes 1572872 | tf_op jit(solution)/shard_map/ppermute | solution.py:366
  7.5 9.0 %collective-permute-start.2 = (bf16[256,1024]{1,0:T(8,128)(2,1)S(1)}, bf16[256,1024]{1,0:T(8,128)(2,1)}, u32[]{:S(2)}, u32[]{:S(2)}) collective-permute-start(bf16[256,1024]{1,0:T(8,128)(2,1)S(1)} %bitcast.34), channel_id=1, source_target_pairs={{0,1},{1,0},{2,3},{3,2},{4,5},{5,4},{6,7},{7,6},{8,9},{9,8},{10,11... | collective-permute-start | bytes 1572872 | tf_op jit(solution)/shard_map/ppermute | solution.py:366
  11.5 21.3 %collective-permute-start.7 = (bf16[1,2,512,256]{3,2,1,0:T(8,128)(2,1)}, bf16[1,2,512,256]{3,2,1,0:T(8,128)(2,1)}, u32[]{:S(2)}, u32[]{:S(2)}) collective-permute-start(bf16[1,2,512,256]{3,2,1,0:T(8,128)(2,1)} %get-tuple-element.107), channel_id=1, source_target_pairs={{0,4},{4,0},{8,12},{12,8},{16,20},{20,16},{24,28},{28,24},{1,5},{5... | collective-permute-start | bytes 1572872 | tf_op jit(solution)/shard_map/ppermute | solution.py:370
  15.9 15.2 %collective-permute-start.8 = (bf16[256,1024]{1,0:T(8,128)(2,1)S(1)}, bf16[256,1024]{1,0:T(8,128)(2,1)S(1)}, u32[]{:S(2)}, u32[]{:S(2)}) collective-permute-start(bf16[256,1024]{1,0:T(8,128)(2,1)S(1)} %bitcast.35), channel_id=1, source_target_pairs={{0,2},{1,3},{2,0},{3,1},{4,6},{5,7},{6,4},{7,5},{8,10},{9,11},{10,... | collective-permute-start | bytes 1572872 | tf_op jit(solution)/shard_map/ppermute | solution.py:368
  18.6 13.3 %copy-start.7 = (bf16[512,256]{1,0:T(8,128)(2,1)}, bf16[512,256]{1,0:T(8,128)(2,1)S(1)}, u32[]{:S(2)}) copy-start(bf16[512,256]{1,0:T(8,128)(2,1)S(1)} %get-tuple-element.110.ahead) | copy-start | bytes 786436
  20.2 2.1 %collective-permute-start.3 = (bf16[256,1024]{1,0:T(8,128)(2,1)}, bf16[256,1024]{1,0:T(8,128)(2,1)S(1)}, u32[]{:S(2)}, u32[]{:S(2)}) collective-permute-start(bf16[256,1024]{1,0:T(8,128)(2,1)} %collective-permute-done.refs_0_.refs_2_), channel_id=1, source_target_pairs={{0,1},{1,0},{2,3},{3,2},{4,5},{5,4},{6,7},{7,6},{8,9},{9,8},{10,11... | collective-permute-start | bytes 1572872 | tf_op jit(solution)/shard_map/ppermute | solution.py:375
  22.3 9.6 %copy-start.5 = (bf16[256,1024]{1,0:T(8,128)(2,1)}, bf16[256,1024]{1,0:T(8,128)(2,1)S(1)}, u32[]{:S(2)}) copy-start(bf16[256,1024]{1,0:T(8,128)(2,1)S(1)} %collective-permute-done.3.refs_1_.refs_3_) | copy-start | bytes 1572868
  24.1 15.8 %collective-permute-start.5 = (bf16[1024,256]{1,0:T(8,128)(2,1)S(1)}, bf16[1024,256]{1,0:T(8,128)(2,1)}, u32[]{:S(2)}, u32[]{:S(2)}) collective-permute-start(bf16[1024,256]{1,0:T(8,128)(2,1)S(1)} %project.6.refs_0_.refs_6_), channel_id=1, source_target_pairs={{0,8},{4,12},{8,0},{12,4},{16,24},{20,28},{24,16},{28,20},{1,9},{5... | collective-permute-start | bytes 1572872 | tf_op jit(solution)/shard_map/ppermute | solution.py:407
  26.2 15.5 %collective-permute-start.6 = (bf16[1024,256]{1,0:T(8,128)(2,1)S(1)}, bf16[1024,256]{1,0:T(8,128)(2,1)}, u32[]{:S(2)}, u32[]{:S(2)}) collective-permute-start(bf16[1024,256]{1,0:T(8,128)(2,1)S(1)} %project.6.refs_0_.refs_6_), channel_id=1, source_target_pairs={{8,16},{16,8},{12,20},{20,12},{9,17},{17,9},{13,21},{21,13},{10,18... | collective-permute-start | bytes 1572872 | tf_op jit(solution)/shard_map/ppermute | solution.py:408
  27.7 14.0 %collective-permute-start.4 = (bf16[1,2,512,256]{3,2,1,0:T(8,128)(2,1)}, bf16[1,2,512,256]{3,2,1,0:T(8,128)(2,1)}, u32[]{:S(2)}, u32[]{:S(2)}) collective-permute-start(bf16[1,2,512,256]{3,2,1,0:T(8,128)(2,1)} %get-tuple-element.104), channel_id=1, source_target_pairs={{0,4},{4,0},{8,12},{12,8},{16,20},{20,16},{24,28},{28,24},{1,5},{5... | collective-permute-start | bytes 1572872 | tf_op jit(solution)/shard_map/ppermute | solution.py:406
  32.7 5.6 %collective-permute-start.10 = (bf16[128,1024]{1,0:T(8,128)(2,1)}, bf16[128,1024]{1,0:T(8,128)(2,1)S(1)}, u32[]{:S(2)}, u32[]{:S(2)}) collective-permute-start(bf16[128,1024]{1,0:T(8,128)(2,1)} %get-tuple-element.212), channel_id=1, source_target_pairs={{0,1},{1,0},{2,3},{3,2},{4,5},{5,4},{6,7},{7,6},{8,9},{9,8},{10,11... | collective-permute-start | bytes 786440 | tf_op jit(solution)/shard_map/ppermute | solution.py:412
  32.7 5.6 %collective-permute-start.9 = (bf16[128,1024]{1,0:T(8,128)(2,1)}, bf16[128,1024]{1,0:T(8,128)(2,1)}, u32[]{:S(2)}, u32[]{:S(2)}) collective-permute-start(bf16[128,1024]{1,0:T(8,128)(2,1)} %get-tuple-element.213), channel_id=1, source_target_pairs={{0,1},{1,0},{2,3},{3,2},{4,5},{5,4},{6,7},{7,6},{8,9},{9,8},{10,11... | collective-permute-start | bytes 786440 | tf_op jit(solution)/shard_map/ppermute | solution.py:412
  33.6 4.7 %copy-start.3 = (bf16[256,1024]{1,0:T(8,128)(2,1)S(1)}, bf16[256,1024]{1,0:T(8,128)(2,1)}, u32[]{:S(2)}) copy-start(bf16[256,1024]{1,0:T(8,128)(2,1)} %copy-done.2) | copy-start | bytes 1572868
  41.8 10.0 %copy-start.1 = (bf16[256,1,1024]{2,0,1:T(8,128)(2,1)S(1)}, bf16[256,1,1024]{2,0,1:T(8,128)(2,1)}, u32[]{:S(2)}) copy-start(bf16[256,1,1024]{2,0,1:T(8,128)(2,1)} %copy-done) | copy-start | bytes 1572868
  41.8 10.0 %copy-start.6 = (bf16[256,1024]{1,0:T(8,128)(2,1)S(1)}, bf16[256,1024]{1,0:T(8,128)(2,1)}, u32[]{:S(2)}) copy-start(bf16[256,1024]{1,0:T(8,128)(2,1)} %copy-done.5) | copy-start | bytes 1572868
  41.8 15.2 %collective-permute-start.12 = (bf16[1024,256]{1,0:T(8,128)(2,1)S(1)}, bf16[1024,256]{1,0:T(8,128)(2,1)S(1)}, u32[]{:S(2)}, u32[]{:S(2)}) collective-permute-start(bf16[1024,256]{1,0:T(8,128)(2,1)S(1)} %broadcast_select_fusion.5), channel_id=1, source_target_pairs={{0,8},{4,12},{8,0},{12,4},{16,24},{20,28},{24,16},{28,20},{1,9},{5... | collective-permute-start | bytes 1572872 | tf_op jit(solution)/shard_map/ppermute | solution.py:407
  46.3 12.2 %collective-permute-start.11 = (bf16[1,2,512,256]{3,2,1,0:T(8,128)(2,1)S(1)}, bf16[1,2,512,256]{3,2,1,0:T(8,128)(2,1)S(1)}, u32[]{:S(2)}, u32[]{:S(2)}) collective-permute-start(bf16[1,2,512,256]{3,2,1,0:T(8,128)(2,1)S(1)} %get-tuple-element.111), channel_id=1, source_target_pairs={{0,4},{4,0},{8,12},{12,8},{16,20},{20,16},{24,28},{28,24},{1,5},{5... | collective-permute-start | bytes 1572872 | tf_op jit(solution)/shard_map/ppermute | solution.py:406
  47.8 10.7 %collective-permute-start.13 = (bf16[1024,256]{1,0:T(8,128)(2,1)}, bf16[1024,256]{1,0:T(8,128)(2,1)S(1)}, u32[]{:S(2)}, u32[]{:S(2)}) collective-permute-start(bf16[1024,256]{1,0:T(8,128)(2,1)} %collective-permute-done.5.refs_0_.refs_1_), channel_id=1, source_target_pairs={{8,16},{16,8},{12,20},{20,12},{9,17},{17,9},{13,21},{21,13},{10,18... | collective-permute-start | bytes 1572872 | tf_op jit(solution)/shard_map/ppermute | solution.py:408
  58.6 13.3 %collective-permute-start.15 = (bf16[1024,256]{1,0:T(8,128)(2,1)S(1)}, bf16[1024,256]{1,0:T(8,128)(2,1)S(1)}, u32[]{:S(2)}, u32[]{:S(2)}) collective-permute-start(bf16[1024,256]{1,0:T(8,128)(2,1)S(1)} %broadcast_select_fusion.4), channel_id=1, source_target_pairs={{0,8},{4,12},{8,0},{12,4},{16,24},{20,28},{24,16},{28,20},{1,9},{5... | collective-permute-start | bytes 1572872 | tf_op jit(solution)/shard_map/ppermute | solution.py:407
  62.3 11.0 %collective-permute-start.14 = (bf16[1,2,512,256]{3,2,1,0:T(8,128)(2,1)S(1)}, bf16[1,2,512,256]{3,2,1,0:T(8,128)(2,1)S(1)}, u32[]{:S(2)}, u32[]{:S(2)}) collective-permute-start(bf16[1,2,512,256]{3,2,1,0:T(8,128)(2,1)S(1)} %get-tuple-element.124), channel_id=1, source_target_pairs={{0,4},{4,0},{8,12},{12,8},{16,20},{20,16},{24,28},{28,24},{1,5},{5... | collective-permute-start | bytes 1572872 | tf_op jit(solution)/shard_map/ppermute | solution.py:406
  62.8 10.5 %collective-permute-start.16 = (bf16[1024,256]{1,0:T(8,128)(2,1)S(1)}, bf16[1024,256]{1,0:T(8,128)(2,1)S(1)}, u32[]{:S(2)}, u32[]{:S(2)}) collective-permute-start(bf16[1024,256]{1,0:T(8,128)(2,1)S(1)} %collective-permute-done.12.refs_0_.refs_1_), channel_id=1, source_target_pairs={{8,16},{16,8},{12,20},{20,12},{9,17},{17,9},{13,21},{21,13},{10,18... | collective-permute-start | bytes 1572872 | tf_op jit(solution)/shard_map/ppermute | solution.py:408
  67.8 10.4 %copy-start.4 = (bf16[256,1024]{1,0:T(8,128)(2,1)S(1)}, bf16[256,1024]{1,0:T(8,128)(2,1)}, u32[]{:S(2)}) copy-start(bf16[256,1024]{1,0:T(8,128)(2,1)} %refs_4_.1) | copy-start | bytes 1572868
  73.4 10.9 %collective-permute-start.17 = (bf16[1024,256]{1,0:T(8,128)(2,1)S(1)}, bf16[1024,256]{1,0:T(8,128)(2,1)S(1)}, u32[]{:S(2)}, u32[]{:S(2)}) collective-permute-start(bf16[1024,256]{1,0:T(8,128)(2,1)S(1)} %broadcast_select_fusion.3), channel_id=1, source_target_pairs={{0,8},{4,12},{8,0},{12,4},{16,24},{20,28},{24,16},{28,20},{1,9},{5... | collective-permute-start | bytes 1572872 | tf_op jit(solution)/shard_map/ppermute | solution.py:407
  75.9 8.4 %collective-permute-start.18 = (bf16[1024,256]{1,0:T(8,128)(2,1)S(1)}, bf16[1024,256]{1,0:T(8,128)(2,1)S(1)}, u32[]{:S(2)}, u32[]{:S(2)}) collective-permute-start(bf16[1024,256]{1,0:T(8,128)(2,1)S(1)} %project.7.refs_0_.refs_6_), channel_id=1, source_target_pairs={{8,16},{16,8},{12,20},{20,12},{9,17},{17,9},{13,21},{21,13},{10,18... | collective-permute-start | bytes 1572872 | tf_op jit(solution)/shard_map/ppermute | solution.py:408
  76.6 14.7 %collective-permute-start.21 = (bf16[1,2,512,256]{3,2,1,0:T(8,128)(2,1)S(1)}, bf16[1,2,512,256]{3,2,1,0:T(8,128)(2,1)S(1)}, u32[]{:S(2)}, u32[]{:S(2)}) collective-permute-start(bf16[1,2,512,256]{3,2,1,0:T(8,128)(2,1)S(1)} %get-tuple-element.148), channel_id=1, source_target_pairs={{0,4},{4,0},{8,12},{12,8},{16,20},{20,16},{24,28},{28,24},{1,5},{5... | collective-permute-start | bytes 1572872 | tf_op jit(solution)/shard_map/ppermute | solution.py:406
  78.2 18.8 %collective-permute-start.26 = (bf16[256,1024]{1,0:T(8,128)(2,1)S(1)}, bf16[256,1024]{1,0:T(8,128)(2,1)S(1)}, u32[]{:S(2)}, u32[]{:S(2)}) collective-permute-start(bf16[256,1024]{1,0:T(8,128)(2,1)S(1)} %copy-done.4), channel_id=1, source_target_pairs={{0,2},{1,3},{2,0},{3,1},{4,6},{5,7},{6,4},{7,5},{8,10},{9,11},{10,... | collective-permute-start | bytes 1572872 | tf_op jit(solution)/shard_map/ppermute | solution.py:393
  84.5 12.8 %collective-permute-start.20 = (bf16[1024,256]{1,0:T(8,128)(2,1)S(1)}, bf16[1024,256]{1,0:T(8,128)(2,1)S(1)}, u32[]{:S(2)}, u32[]{:S(2)}) collective-permute-start(bf16[1024,256]{1,0:T(8,128)(2,1)S(1)} %add.1011), channel_id=1, source_target_pairs={{8,16},{16,8},{12,20},{20,12},{9,17},{17,9},{13,21},{21,13},{10,18... | collective-permute-start | bytes 1572872 | tf_op jit(solution)/shard_map/ppermute | solution.py:408
  85.2 13.6 %collective-permute-start.19 = (bf16[1024,256]{1,0:T(8,128)(2,1)S(1)}, bf16[1024,256]{1,0:T(8,128)(2,1)S(1)}, u32[]{:S(2)}, u32[]{:S(2)}) collective-permute-start(bf16[1024,256]{1,0:T(8,128)(2,1)S(1)} %broadcast_select_fusion.2), channel_id=1, source_target_pairs={{0,8},{4,12},{8,0},{12,4},{16,24},{20,28},{24,16},{28,20},{1,9},{5... | collective-permute-start | bytes 1572872 | tf_op jit(solution)/shard_map/ppermute | solution.py:407
  91.3 20.0 %collective-permute-start.25 = (bf16[256,1024]{1,0:T(8,128)(2,1)S(1)}, bf16[256,1024]{1,0:T(8,128)(2,1)S(1)}, u32[]{:S(2)}, u32[]{:S(2)}) collective-permute-start(bf16[256,1024]{1,0:T(8,128)(2,1)S(1)} %copy-done.4), channel_id=1, source_target_pairs={{0,1},{1,0},{2,3},{3,2},{4,5},{5,4},{6,7},{7,6},{8,9},{9,8},{10,11... | collective-permute-start | bytes 1572872 | tf_op jit(solution)/shard_map/ppermute | solution.py:393
  91.3 14.3 %collective-permute-start.24 = (bf16[1,2,512,256]{3,2,1,0:T(8,128)(2,1)S(1)}, bf16[1,2,512,256]{3,2,1,0:T(8,128)(2,1)S(1)}, u32[]{:S(2)}, u32[]{:S(2)}) collective-permute-start(bf16[1,2,512,256]{3,2,1,0:T(8,128)(2,1)S(1)} %get-tuple-element.153), channel_id=1, source_target_pairs={{0,4},{4,0},{8,12},{12,8},{16,20},{20,16},{24,28},{28,24},{1,5},{5... | collective-permute-start | bytes 1572872 | tf_op jit(solution)/shard_map/ppermute | solution.py:406
  97.0 14.3 %collective-permute-start.27 = (bf16[256,1024]{1,0:T(8,128)(2,1)S(1)}, bf16[256,1024]{1,0:T(8,128)(2,1)S(1)}, u32[]{:S(2)}, u32[]{:S(2)}) collective-permute-start(bf16[256,1024]{1,0:T(8,128)(2,1)S(1)} %collective-permute-done.26.refs_6_), channel_id=1, source_target_pairs={{0,1},{1,0},{2,3},{3,2},{4,5},{5,4},{6,7},{7,6},{8,9},{9,8},{10,11... | collective-permute-start | bytes 1572872 | tf_op jit(solution)/shard_map/ppermute | solution.py:422
  98.9 12.4 %collective-permute-start.23 = (bf16[1024,256]{1,0:T(8,128)(2,1)S(1)}, bf16[1024,256]{1,0:T(8,128)(2,1)S(1)}, u32[]{:S(2)}, u32[]{:S(2)}) collective-permute-start(bf16[1024,256]{1,0:T(8,128)(2,1)S(1)} %add.1012), channel_id=1, source_target_pairs={{8,16},{16,8},{12,20},{20,12},{9,17},{17,9},{13,21},{21,13},{10,18... | collective-permute-start | bytes 1572872 | tf_op jit(solution)/shard_map/ppermute | solution.py:408
  99.7 12.7 %collective-permute-start.22 = (bf16[1024,256]{1,0:T(8,128)(2,1)S(1)}, bf16[1024,256]{1,0:T(8,128)(2,1)S(1)}, u32[]{:S(2)}, u32[]{:S(2)}) collective-permute-start(bf16[1024,256]{1,0:T(8,128)(2,1)S(1)} %broadcast_select_fusion.1), channel_id=1, source_target_pairs={{0,8},{4,12},{8,0},{12,4},{16,24},{20,28},{24,16},{28,20},{1,9},{5... | collective-permute-start | bytes 1572872 | tf_op jit(solution)/shard_map/ppermute | solution.py:407
  105.7 14.8 %collective-permute-start.30 = (bf16[1,2,512,256]{3,2,1,0:T(8,128)(2,1)S(1)}, bf16[1,2,512,256]{3,2,1,0:T(8,128)(2,1)S(1)}, u32[]{:S(2)}, u32[]{:S(2)}) collective-permute-start(bf16[1,2,512,256]{3,2,1,0:T(8,128)(2,1)S(1)} %get-tuple-element.160), channel_id=1, source_target_pairs={{0,4},{4,0},{8,12},{12,8},{16,20},{20,16},{24,28},{28,24},{1,5},{5... | collective-permute-start | bytes 1572872 | tf_op jit(solution)/shard_map/ppermute | solution.py:406
  112.5 12.1 %collective-permute-start.29 = (bf16[1024,256]{1,0:T(8,128)(2,1)S(1)}, bf16[1024,256]{1,0:T(8,128)(2,1)S(1)}, u32[]{:S(2)}, u32[]{:S(2)}) collective-permute-start(bf16[1024,256]{1,0:T(8,128)(2,1)S(1)} %add.1014), channel_id=1, source_target_pairs={{8,16},{16,8},{12,20},{20,12},{9,17},{17,9},{13,21},{21,13},{10,18... | collective-permute-start | bytes 1572872 | tf_op jit(solution)/shard_map/ppermute | solution.py:408
  113.3 12.3 %collective-permute-start.28 = (bf16[1024,256]{1,0:T(8,128)(2,1)S(1)}, bf16[1024,256]{1,0:T(8,128)(2,1)S(1)}, u32[]{:S(2)}, u32[]{:S(2)}) collective-permute-start(bf16[1024,256]{1,0:T(8,128)(2,1)S(1)} %add_select_fusion.1), channel_id=1, source_target_pairs={{0,8},{4,12},{8,0},{12,4},{16,24},{20,28},{24,16},{28,20},{1,9},{5... | collective-permute-start | bytes 1572872 | tf_op jit(solution)/shard_map/ppermute | solution.py:407
  117.7 16.8 %collective-permute-start.33 = (bf16[1,2,512,256]{3,2,1,0:T(8,128)(2,1)S(1)}, bf16[1,2,512,256]{3,2,1,0:T(8,128)(2,1)S(1)}, u32[]{:S(2)}, u32[]{:S(2)}) collective-permute-start(bf16[1,2,512,256]{3,2,1,0:T(8,128)(2,1)S(1)} %get-tuple-element.164), channel_id=1, source_target_pairs={{0,4},{4,0},{8,12},{12,8},{16,20},{20,16},{24,28},{28,24},{1,5},{5... | collective-permute-start | bytes 1572872 | tf_op jit(solution)/shard_map/ppermute | solution.py:406
  125.7 15.4 %collective-permute-start.32 = (bf16[1024,256]{1,0:T(8,128)(2,1)S(1)}, bf16[1024,256]{1,0:T(8,128)(2,1)S(1)}, u32[]{:S(2)}, u32[]{:S(2)}) collective-permute-start(bf16[1024,256]{1,0:T(8,128)(2,1)S(1)} %get-tuple-element.211), channel_id=1, source_target_pairs={{8,16},{16,8},{12,20},{20,12},{9,17},{17,9},{13,21},{21,13},{10,18... | collective-permute-start | bytes 1572872 | tf_op jit(solution)/shard_map/ppermute | solution.py:408
  126.5 14.6 %collective-permute-start.31 = (bf16[1024,256]{1,0:T(8,128)(2,1)S(1)}, bf16[1024,256]{1,0:T(8,128)(2,1)S(1)}, u32[]{:S(2)}, u32[]{:S(2)}) collective-permute-start(bf16[1024,256]{1,0:T(8,128)(2,1)S(1)} %add_select_fusion), channel_id=1, source_target_pairs={{0,8},{4,12},{8,0},{12,4},{16,24},{20,28},{24,16},{28,20},{1,9},{5... | collective-permute-start | bytes 1572872 | tf_op jit(solution)/shard_map/ppermute | solution.py:407
  132.9 6.5 %collective-permute-start.35 = (bf16[256,256]{1,0:T(8,128)(2,1)S(1)}, bf16[256,256]{1,0:T(8,128)(2,1)S(1)}, u32[]{:S(2)}, u32[]{:S(2)}) collective-permute-start(bf16[256,256]{1,0:T(8,128)(2,1)S(1)} %get-tuple-element.172), channel_id=1, source_target_pairs={{0,2},{1,3},{2,0},{3,1},{4,6},{5,7},{6,4},{7,5},{8,10},{9,11},{10,... | collective-permute-start | bytes 393224 | tf_op jit(solution)/shard_map/ppermute | solution.py:331
  134.5 5.8 %collective-permute-start.36 = (bf16[256,256]{1,0:T(8,128)(2,1)S(1)}, bf16[256,256]{1,0:T(8,128)(2,1)S(1)}, u32[]{:S(2)}, u32[]{:S(2)}) collective-permute-start(bf16[256,256]{1,0:T(8,128)(2,1)S(1)} %get-tuple-element.173), channel_id=1, source_target_pairs={{0,3},{1,2},{2,1},{3,0},{4,7},{5,6},{6,5},{7,4},{8,11},{9,10},{10,... | collective-permute-start | bytes 393224 | tf_op jit(solution)/shard_map/ppermute | solution.py:331
  134.5 5.8 %copy-start.9 = (f32[1024]{0:T(1024)S(1)}, f32[1024]{0:T(1024)}, u32[]{:S(2)}) copy-start(f32[1024]{0:T(1024)} %param.16) | copy-start | bytes 12292
  134.5 5.8 %collective-permute-start.34 = (bf16[256,256]{1,0:T(8,128)(2,1)S(1)}, bf16[256,256]{1,0:T(8,128)(2,1)S(1)}, u32[]{:S(2)}, u32[]{:S(2)}) collective-permute-start(bf16[256,256]{1,0:T(8,128)(2,1)S(1)} %get-tuple-element.171), channel_id=1, source_target_pairs={{0,1},{1,0},{2,3},{3,2},{4,5},{5,4},{6,7},{7,6},{8,9},{9,8},{10,11... | collective-permute-start | bytes 393224 | tf_op jit(solution)/shard_map/ppermute | solution.py:331
  142.2 6.4 %collective-permute-start.38 = (bf16[256,256]{1,0:T(8,128)(2,1)S(1)}, bf16[256,256]{1,0:T(8,128)(2,1)S(1)}, u32[]{:S(2)}, u32[]{:S(2)}) collective-permute-start(bf16[256,256]{1,0:T(8,128)(2,1)S(1)} %get-tuple-element.188), channel_id=1, source_target_pairs={{0,2},{1,3},{2,0},{3,1},{4,6},{5,7},{6,4},{7,5},{8,10},{9,11},{10,... | collective-permute-start | bytes 393224 | tf_op jit(solution)/shard_map/ppermute | solution.py:331
  143.0 7.2 %collective-permute-start.39 = (bf16[256,256]{1,0:T(8,128)(2,1)S(1)}, bf16[256,256]{1,0:T(8,128)(2,1)S(1)}, u32[]{:S(2)}, u32[]{:S(2)}) collective-permute-start(bf16[256,256]{1,0:T(8,128)(2,1)S(1)} %get-tuple-element.189), channel_id=1, source_target_pairs={{0,3},{1,2},{2,1},{3,0},{4,7},{5,6},{6,5},{7,4},{8,11},{9,10},{10,... | collective-permute-start | bytes 393224 | tf_op jit(solution)/shard_map/ppermute | solution.py:331
  145.0 5.1 %collective-permute-start.37 = (bf16[256,256]{1,0:T(8,128)(2,1)S(1)}, bf16[256,256]{1,0:T(8,128)(2,1)S(1)}, u32[]{:S(2)}, u32[]{:S(2)}) collective-permute-start(bf16[256,256]{1,0:T(8,128)(2,1)S(1)} %get-tuple-element.187), channel_id=1, source_target_pairs={{0,1},{1,0},{2,3},{3,2},{4,5},{5,4},{6,7},{7,6},{8,9},{9,8},{10,11... | collective-permute-start | bytes 393224 | tf_op jit(solution)/shard_map/ppermute | solution.py:331
  (5 other events, 14.6 us)
